TPU v7x, 32 devices: a whole 2x2x4 slice. The times are simulated.
32 devices in a mesh: ens: 2 (over y), tile: 4 (over z), trc: 2 (over x), lev: 2 (over core).
Axes of the slice: x: 2, y: 2, z: 4, core: 2. Of those that a mesh axis runs over, the one named last changes fastest.
Arguments:
- tracers: float32 [32, 16, 64, 128], P('trc', 'lev', ('ens', 'tile')), parts along dimension 2, may hold values from -6 to 6
- cotangent: float32 [32, 16, 64, 128], P('trc', 'lev', ('ens', 'tile')), parts along dimension 2, may hold values from -3 to 3
- zonal_speed: float32 [16, 64, 128], P('lev', ('ens', 'tile')), parts along dimension 1, may hold values from -0.3 to 0.3
- meridional_speed: float32 [16, 64, 128], P('lev', ('ens', 'tile')), parts along dimension 1, may hold values from -0.3 to 0.3
- vertical_speed: float32 [16, 64, 128], P('lev', ('ens', 'tile')), parts along dimension 1, may hold values from -0.3 to 0.3
- lateral_mixing: float32 [16, 64, 128], P('lev', ('ens', 'tile')), parts along dimension 1, may hold values from 0.01 to 0.08
- vertical_mixing: float32 [16, 64, 128], P('lev', ('ens', 'tile')), parts along dimension 1, may hold values from 0.02 to 0.16
- column_depth: int32 [64, 128], P(('ens', 'tile')), parts along dimension 0, may hold values from 0 to 16
Outputs:
- start_cotangent: float32 [32, 16, 64, 128], P('trc', 'lev', ('ens', 'tile')), parts along dimension 2
- speed_cotangent: float32 [3, 16, 64, 128], P(None, ('lev', 'trc'), ('ens', 'tile')), parts along dimension 2
There are 2 independent parts, one for each index of `ens`. A program takes and returns all parts, laid end to end along the dimension named above; each array names one. Nothing has to cross between parts.
All inputs are finite; a program needn't handle non-finite values.
Results may differ from a plain program's by a relative error of at most 0.0003.
Values sent between devices are 32-bit elements; how exact they have to be, the bound alone decides.
A program may use at most 64 MiB of HBM per device.

v0:
```python
import jax
import jax.numpy as jnp
from jax import lax
from jax.sharding import PartitionSpec as P

albada_floor = 0.01


def padded_2(block, sides, width):
    for axis, dim in sides:
        count = lax.axis_size(axis)
        forward = [(i, i + 1) for i in range(count - 1)]
        backward = [(target, source) for source, target in forward]
        low = lax.ppermute(
            lax.slice_in_dim(block, block.shape[dim] - width, None, axis=dim), axis, forward
        )
        high = lax.ppermute(lax.slice_in_dim(block, 0, width, axis=dim), axis, backward)
        block = jnp.concatenate([low, block, high], axis=dim)
    return block


def albada(lower_step, upper_step):
    return (
        lower_step
        * upper_step
        * (lower_step + upper_step)
        / (lower_step * lower_step + upper_step * upper_step + albada_floor)
    )


def face_flux(far_behind, behind, beyond, far_beyond, velocity, spread, opened):
    rising = behind + 0.5 * albada(behind - far_behind, beyond - behind)
    falling = beyond - 0.5 * albada(beyond - behind, far_beyond - beyond)
    carried = jnp.where(velocity >= 0.0, rising, falling)
    return opened * (velocity * carried - spread * (beyond - behind))


def shift_across(values, offset):
    if offset > 0:
        filler = jnp.zeros(values.shape[:-1] + (offset,), values.dtype)
        return jnp.concatenate([filler, values[..., :-offset]], axis=-1)
    filler = jnp.zeros(values.shape[:-1] + (-offset,), values.dtype)
    return jnp.concatenate([values[..., -offset:], filler], axis=-1)


def window(values, direction, offset):
    leading = values.ndim - 3
    pieces = [slice(None)] * leading
    for spatial in range(2):
        extent = values.shape[leading + spatial] - 4
        if spatial == direction:
            pieces.append(slice(offset, extent + 1 + offset))
        else:
            pieces.append(slice(2, extent + 2))
    pieces.append(slice(None))
    return values[tuple(pieces)]


def advance(padded, fields):
    wetness = fields[5]
    centre = padded[:, 2:-2, 2:-2, :]
    result = centre
    for direction, speed_row, spread_row in ((0, 2, 4), (1, 0, 3)):
        through = face_flux(
            window(padded, direction, 0),
            window(padded, direction, 1),
            window(padded, direction, 2),
            window(padded, direction, 3),
            window(fields[speed_row], direction, 2),
            window(fields[spread_row], direction, 2),
            window(wetness, direction, 1) * window(wetness, direction, 2),
        )
        extent = through.shape[direction + 1]
        result = (
            result
            + lax.slice_in_dim(through, 0, extent - 1, axis=direction + 1)
            - lax.slice_in_dim(through, 1, extent, axis=direction + 1)
        )
    centre_fields = fields[:, 2:-2, 2:-2, :]
    inner_wet = centre_fields[5]
    through = face_flux(
        shift_across(centre, 2),
        shift_across(centre, 1),
        centre,
        shift_across(centre, -1),
        centre_fields[1],
        centre_fields[3],
        shift_across(inner_wet, 1) * inner_wet,
    )
    return result + through - shift_across(through, -1)


def local_step(tracer_part, field_part):
    fields = jnp.pad(field_part, ((0, 0), (1, 1), (1, 1), (0, 0)))
    return advance(tracer_part, fields)


def fold_edges(gathered):
    levels = gathered.shape[1] - 4
    columns = gathered.shape[2] - 4
    beside_all = padded_2(gathered, (("tile", 2), ("lev", 1)), 2)
    owned_part = gathered[:, 2:-2, 2:-2]
    owned_part = owned_part.at[:, 0:2].add(beside_all[:, 0:2, 4 : columns + 4])
    owned_part = owned_part.at[:, levels - 2 : levels].add(
        beside_all[:, levels + 6 : levels + 8, 4 : columns + 4]
    )
    owned_part = owned_part.at[:, :, 0:2].add(beside_all[:, 4 : levels + 4, 0:2])
    owned_part = owned_part.at[:, :, columns - 2 : columns].add(
        beside_all[:, 4 : levels + 4, columns + 6 : columns + 8]
    )
    return owned_part


def fold_back(tracer_cot, speed_cot, tracer_count):
    combined = jnp.concatenate([tracer_cot, jnp.pad(speed_cot, ((0, 0), (1, 1), (1, 1), (0, 0)))])
    owned_part = fold_edges(combined)
    return (owned_part[:tracer_count], owned_part[tracer_count:])


def share_speeds(values):
    return lax.psum_scatter(values, "trc", scatter_dimension=1, tiled=True)


def body(
    tracers,
    cotangent,
    zonal_speed,
    meridional_speed,
    vertical_speed,
    lateral_mixing,
    vertical_mixing,
    column_depth,
):
    tracer_count = tracers.shape[0]
    levels = tracers.shape[1]
    first_level = lax.axis_index("lev") * levels
    wetness = (
        (first_level + jnp.arange(levels, dtype=jnp.int32))[:, None, None] < column_depth[None]
    ).astype(jnp.float32)
    fields = jnp.stack(
        [zonal_speed, meridional_speed, vertical_speed, lateral_mixing, vertical_mixing, wetness]
    )
    deep_fields = padded_2(fields, (("tile", 2), ("lev", 1)), 3)
    deep_tracers = padded_2(tracers, (("tile", 2), ("lev", 1)), 4)
    rim_fields = deep_fields[:, 2:-2, 2:-2]
    early_rims = deep_tracers[:, 2:-2, 2:-2]
    late_rims = advance(deep_tracers, jnp.pad(deep_fields, ((0, 0), (1, 1), (1, 1), (0, 0))))
    speed_rims = rim_fields[0:3]
    other_rims = rim_fields[3:6]

    def rim_stepper(tracer_part, speed_part):
        return local_step(tracer_part, jnp.concatenate([speed_part, other_rims]))

    _, pull_late = jax.vjp(rim_stepper, late_rims, speed_rims)
    late_tracer, late_speed_rims = pull_late(cotangent)
    middle_cot, late_speed = fold_back(late_tracer, late_speed_rims, tracer_count)
    _, pull_early = jax.vjp(rim_stepper, early_rims, speed_rims)
    early_tracer, early_speed_rims = pull_early(middle_cot)
    start_cotangent, early_speed = fold_back(early_tracer, early_speed_rims, tracer_count)
    speed_cotangent = share_speeds(late_speed) + share_speeds(early_speed)
    return (start_cotangent, speed_cotangent)


def solution(mesh):
    return jax.shard_map(
        body,
        mesh=mesh,
        in_specs=(
            P("trc", "lev", ("ens", "tile"), None),
            P("trc", "lev", ("ens", "tile"), None),
            P("lev", ("ens", "tile"), None),
            P("lev", ("ens", "tile"), None),
            P("lev", ("ens", "tile"), None),
            P("lev", ("ens", "tile"), None),
            P("lev", ("ens", "tile"), None),
            P(("ens", "tile"), None),
        ),
        out_specs=(
            P("trc", "lev", ("ens", "tile"), None),
            P(None, ("lev", "trc"), ("ens", "tile"), None),
        ),
        check_vma=False,
    )
```

profile of v0, /device:TPU:0, one launch (start us, length us, event | category | flops | bytes accessed | tf_op | source)
XLA Modules:
  0.0 133.1 jit_solution(10074227495728779570)
XLA Ops:
  7.3 1.4 %fusion.80 = (f32[16,8,4,128]{3,2,1,0:T(4,128)S(1)}, f32[16,8,4,128]{3,2,1,0:T(4,128)S(1)}) fusion(f32[16,8,8,128]{3,2,1,0:T(8,128)} %param.24), kind=kLoop, calls=%fused_computation.355 | loop fusion | bytes 1048576 | tf_op jit(solution)/shard_map/slice | solution.py:17
  8.9 4.9 %collective-permute-start.5 = (f32[16,8,4,128]{3,0,2,1:T(8,128)S(1)}, f32[16,8,4,128]{3,0,2,1:T(8,128)S(1)}, u32[]{:S(2)}, u32[]{:S(2)}) collective-permute-start(f32[16,8,4,128]{3,0,2,1:T(8,128)S(1)} %copy.67), channel_id=1, source_target_pairs={{0,4},{4,8},{8,12},{1,5},{5,9},{9,13},{2,6},{6,10},{10,14},{3,7},{... | collective-permute-start | bytes 786440 | tf_op jit(solution)/shard_map/ppermute | solution.py:14
  14.0 1.3 collective-permute-start
  15.5 1.4 %collective-permute-start.2 = (f32[6,8,3,128]{3,2,1,0:T(4,128)S(1)}, f32[6,8,3,128]{3,2,1,0:T(4,128)S(1)}, u32[]{:S(2)}, u32[]{:S(2)}) collective-permute-start(f32[6,8,3,128]{3,2,1,0:T(4,128)S(1)} %get-tuple-element.220), channel_id=1, source_target_pairs={{4,0},{8,4},{12,8},{5,1},{9,5},{13,9},{6,2},{10,6},{14,10},{7,3},{... | collective-permute-start | bytes 221192 | tf_op jit(solution)/shard_map/ppermute | solution.py:17
  17.0 5.2 %collective-permute-start.1 = (f32[6,8,3,128]{3,2,1,0:T(4,128)S(1)}, f32[6,8,3,128]{3,2,1,0:T(4,128)S(1)}, u32[]{:S(2)}, u32[]{:S(2)}) collective-permute-start(f32[6,8,3,128]{3,2,1,0:T(4,128)S(1)} %get-tuple-element.219), channel_id=1, source_target_pairs={{0,4},{4,8},{8,12},{1,5},{5,9},{9,13},{2,6},{6,10},{10,14},{3,7},{... | collective-permute-start | bytes 221192 | tf_op jit(solution)/shard_map/ppermute | solution.py:14
  23.8 2.0 %collective-permute-done.2 = f32[6,8,3,128]{3,2,1,0:T(4,128)S(1)} collective-permute-done((f32[6,8,3,128]{3,2,1,0:T(4,128)S(1)}, f32[6,8,3,128]{3,2,1,0:T(4,128)S(1)}, u32[]{:S(2)}, u32[]{:S(2)}) %collective-permute-start.2) | collective-permute-done | bytes 73760 | tf_op jit(solution)/shard_map/ppermute | solution.py:17
  25.8 1.3 collective-permute-start.4
  27.1 3.0 %collective-permute-start.3 = (f32[6,3,14,128]{3,2,1,0:T(8,128)S(1)}, f32[6,3,14,128]{3,2,1,0:T(8,128)S(1)}, u32[]{:S(2)}, u32[]{:S(2)}) collective-permute-start(f32[6,3,14,128]{3,2,1,0:T(8,128)S(1)} %get-tuple-element.213), channel_id=1, source_target_pairs={{0,1},{2,3},{4,5},{6,7},{8,9},{10,11},{12,13},{14,15},{16,17},{18,... | collective-permute-start | bytes 387080 | tf_op jit(solution)/shard_map/ppermute | solution.py:14
  30.3 0.9 collective-permute-done.3
  31.8 0.7 constant_dynamic-update-slice_fusion.1
  32.6 1.3 collective-permute-start.7
  33.9 3.3 %collective-permute-start.6 = (f32[16,4,16,128]{3,0,2,1:T(8,128)S(1)}, f32[16,4,16,128]{3,0,2,1:T(8,128)S(1)}, u32[]{:S(2)}, u32[]{:S(2)}) collective-permute-start(f32[16,4,16,128]{3,0,2,1:T(8,128)S(1)} %get-tuple-element.184), channel_id=1, source_target_pairs={{0,1},{2,3},{4,5},{6,7},{8,9},{10,11},{12,13},{14,15},{16,17},{18,... | collective-permute-start | bytes 1572872 | tf_op jit(solution)/shard_map/ppermute | solution.py:14
  37.4 1.1 collective-permute-done.6
  39.2 1.5 %subtract_multiply_fusion.4 = f32[16,12,12,128]{3,0,2,1:T(8,128)S(1)} fusion(f32[16,12,12,127]{3,0,2,1:T(8,128)S(1)} %get-tuple-element.169, f32[16,12,12,126]{3,0,2,1:T(8,128)S(1)} %slice.765, f32[16,12,12,127]{3,0,2,1:T(8,128)S(1)} %get-tuple-element.168, f32[16,16,16,128]{3,0,2,1:T(8,128)S(1)} %pad_maximum_fusion, ...), kind=kLoop, calls=%fused_computation.29 | loop fusion | flops 7962624 | bytes 6100992 | tf_op jit(solution)/shard_map/mul | solution.py:35
  41.1 1.3 subtract_multiply_fusion
  42.5 0.9 subtract_multiply_fusion.2
  44.6 0.7 multiply_reduce_fusion.17
  45.3 1.1 fusion.32
  48.4 1.4 %add_add_fusion.10 = (f32[16,9,8,128]{3,0,2,1:T(8,128)S(1)}, f32[16,9,8,128]{3,0,2,1:T(8,128)S(1)}, f32[16,9,8,128]{3,0,2,1:T(8,128)S(1)}, f32[16,9,8,128]{3,0,2,1:T(8,128)S(1)}) fusion(f32[16,9,8,128]{3,0,2,1:T(8,128)S(1)} %get-tuple-element.145, f32[9,8,128]{2,1,0:T(8,128)S(1)} %slice.780, f32[9,8,128]{2,1,0:T(8,128)S(1)} %slice_multiply_fusion.9, ...), kind=kLoop, calls=%fused_computation.122 | loop fusion | flops 10469376 | bytes 6018048 | tf_op jit(solution)/shard_map/transpose(jvp())/add_any | solution.py:32
  49.8 1.2 subtract_select_fusion.1
  51.5 1.4 %add_add_fusion.14 = (f32[16,8,9,128]{3,0,2,1:T(8,128)S(1)}, f32[16,8,9,128]{3,0,2,1:T(8,128)S(1)}, f32[16,8,9,128]{3,0,2,1:T(8,128)S(1)}, f32[16,8,9,128]{3,0,2,1:T(8,128)S(1)}) fusion(f32[16,8,9,128]{3,0,2,1:T(8,128)S(1)} %get-tuple-element.142, f32[8,9,128]{2,1,0:T(8,128)S(1)} %slice.772, f32[8,9,128]{2,1,0:T(8,128)S(1)} %slice_multiply_fusion.4, ...), kind=kLoop, calls=%fused_computation.130 | loop fusion | flops 10469376 | bytes 6018048 | tf_op jit(solution)/shard_map/transpose(jvp())/add_any | solution.py:32
  53.6 0.7 slice_add_fusion.4
  54.3 0.6 add_add_fusion.19
  55.4 1.3 collective-permute-start.9
  56.7 4.6 %collective-permute-start.8 = (f32[19,12,2,128]{3,0,2,1:T(8,128)S(1)}, f32[19,12,2,128]{3,0,2,1:T(8,128)S(1)}, u32[]{:S(2)}, u32[]{:S(2)}) collective-permute-start(f32[19,12,2,128]{3,0,2,1:T(8,128)S(1)} %get-tuple-element.178), channel_id=1, source_target_pairs={{0,4},{4,8},{8,12},{1,5},{5,9},{9,13},{2,6},{6,10},{10,14},{3,7},{... | collective-permute-start | bytes 700424 | tf_op jit(solution)/shard_map/ppermute | solution.py:14
  61.2 5.3 %collective-permute-done.9 = f32[19,12,2,128]{3,0,2,1:T(8,128)S(1)} collective-permute-done((f32[19,12,2,128]{3,0,2,1:T(8,128)S(1)}, f32[19,12,2,128]{3,0,2,1:T(8,128)S(1)}, u32[]{:S(2)}, u32[]{:S(2)}) %collective-permute-start.9) | collective-permute-done | bytes 233504 | tf_op jit(solution)/shard_map/ppermute | solution.py:17
  66.5 1.2 collective-permute-done.8
  67.8 1.3 collective-permute-start.10
  69.1 1.3 collective-permute-start.11
  70.5 2.2 %collective-permute-done.11 = f32[19,2,16,128]{3,0,2,1:T(8,128)S(1)} collective-permute-done((f32[19,2,16,128]{3,0,2,1:T(8,128)S(1)}, f32[19,2,16,128]{3,0,2,1:T(8,128)S(1)}, u32[]{:S(2)}, u32[]{:S(2)}) %collective-permute-start.11) | collective-permute-done | bytes 311328 | tf_op jit(solution)/shard_map/ppermute | solution.py:17
  73.0 0.7 multiply_reduce_fusion.14
  73.7 1.2 fusion.28
  74.9 0.7 fusion.25
  76.4 1.2 add_add_fusion.2
  77.6 0.7 add_add_fusion
  78.9 1.4 %add_add_fusion.6 = (f32[16,8,9,128]{3,0,2,1:T(8,128)S(1)}, f32[16,8,9,128]{3,0,2,1:T(8,128)S(1)}, f32[16,8,9,128]{3,0,2,1:T(8,128)S(1)}, f32[16,8,9,128]{3,0,2,1:T(8,128)S(1)}) fusion(f32[16,8,9,128]{3,0,2,1:T(8,128)S(1)} %get-tuple-element.121, f32[8,9,128]{2,1,0:T(8,128)S(1)} %slice.772, f32[8,9,128]{2,1,0:T(8,128)S(1)} %slice_multiply_fusion.4, ...), kind=kLoop, calls=%fused_computation.106 | loop fusion | flops 10469376 | bytes 6018048 | tf_op jit(solution)/shard_map/transpose(jvp())/add_any | solution.py:32
  81.0 0.7 slice_add_fusion.2
  82.6 1.3 collective-permute-start.13
  83.9 5.0 %collective-permute-start.12 = (f32[19,12,2,128]{3,0,2,1:T(8,128)S(1)}, f32[19,12,2,128]{3,0,2,1:T(8,128)S(1)}, u32[]{:S(2)}, u32[]{:S(2)}) collective-permute-start(f32[19,12,2,128]{3,0,2,1:T(8,128)S(1)} %get-tuple-element.176), channel_id=1, source_target_pairs={{0,4},{4,8},{8,12},{1,5},{5,9},{9,13},{2,6},{6,10},{10,14},{3,7},{... | collective-permute-start | bytes 700424 | tf_op jit(solution)/shard_map/ppermute | solution.py:14
  88.9 5.4 %collective-permute-done.13 = f32[19,12,2,128]{3,0,2,1:T(8,128)S(1)} collective-permute-done((f32[19,12,2,128]{3,0,2,1:T(8,128)S(1)}, f32[19,12,2,128]{3,0,2,1:T(8,128)S(1)}, u32[]{:S(2)}, u32[]{:S(2)}) %collective-permute-start.13) | collective-permute-done | bytes 233504 | tf_op jit(solution)/shard_map/ppermute | solution.py:17
  94.3 1.2 collective-permute-done.12
  95.5 1.3 collective-permute-start.14
  96.9 1.3 collective-permute-start.15
  98.3 2.2 %collective-permute-done.15 = f32[19,2,16,128]{3,0,2,1:T(8,128)S(1)} collective-permute-done((f32[19,2,16,128]{3,0,2,1:T(8,128)S(1)}, f32[19,2,16,128]{3,0,2,1:T(8,128)S(1)}, u32[]{:S(2)}, u32[]{:S(2)}) %collective-permute-start.15) | collective-permute-done | bytes 311328 | tf_op jit(solution)/shard_map/ppermute | solution.py:17
  100.7 0.7 copy.48
  102.6 1.0 copy.49
  103.6 21.2 %all-reduce.89.cloned.1.call-done = f32[3,8,8,128]{3,2,1,0:T(8,128)} async-done(((f32[3,8,8,128]{3,2,1,0:T(8,128)}), f32[3,8,8,128]{3,2,1,0:T(8,128)}) %all-reduce.89.cloned.1.call-update) | async-done | bytes 98320
  124.8 1.4 %constant_dynamic-slice_fusion = f32[3,4,8,128]{3,2,1,0:T(8,128)} fusion(f32[3,8,8,128]{3,2,1,0:T(8,128)} %all-reduce.89.cloned.1.call-done, u32[]{:T(128)S(6)} %multiply.25), kind=kLoop, calls=%fused_computation.346 | loop fusion | bytes 98308
  (137 shorter events, 12.8 us)
Async XLA Ops:
  7.2 15.0 %copy-start = (f32[16,8,8,128]{3,2,1,0:T(8,128)S(1)}, f32[16,8,8,128]{3,2,1,0:T(8,128)}, u32[]{:S(2)}) copy-start(f32[16,8,8,128]{3,2,1,0:T(8,128)} %param.24) | copy-start | bytes 1572868
  7.2 8.1 %copy-start.5 = (f32[8,8,128]{2,1,0:T(8,128)S(1)}, f32[8,8,128]{2,1,0:T(8,128)}, u32[]{:S(2)}) copy-start(f32[8,8,128]{2,1,0:T(8,128)} %param.26) | copy-start | bytes 98308
  7.2 8.1 %copy-start.2 = (f32[8,8,128]{2,1,0:T(8,128)S(1)}, f32[8,8,128]{2,1,0:T(8,128)}, u32[]{:S(2)}) copy-start(f32[8,8,128]{2,1,0:T(8,128)} %param.27) | copy-start | bytes 98308
  7.2 8.1 %copy-start.6 = (f32[8,8,128]{2,1,0:T(8,128)S(1)}, f32[8,8,128]{2,1,0:T(8,128)}, u32[]{:S(2)}) copy-start(f32[8,8,128]{2,1,0:T(8,128)} %param.28) | copy-start | bytes 98308
  7.2 8.2 %copy-start.3 = (f32[8,8,128]{2,1,0:T(8,128)S(1)}, f32[8,8,128]{2,1,0:T(8,128)}, u32[]{:S(2)}) copy-start(f32[8,8,128]{2,1,0:T(8,128)} %param.29) | copy-start | bytes 98308
  7.2 8.2 %copy-start.7 = (f32[8,8,128]{2,1,0:T(8,128)S(1)}, f32[8,8,128]{2,1,0:T(8,128)}, u32[]{:S(2)}) copy-start(f32[8,8,128]{2,1,0:T(8,128)} %param.30) | copy-start | bytes 98308
  7.2 8.2 %copy-start.4 = (s32[8,128]{1,0:T(8,128)S(1)}, s32[8,128]{1,0:T(8,128)}, u32[]{:S(2)}) copy-start(s32[8,128]{1,0:T(8,128)} %param.31) | copy-start | bytes 12292
  7.2 117.6 %all-reduce.89.cloned.1.call-start = ((), (), s32[]{:S(2)}) async-start(), calls=%async_computation | async-start | bytes 196608
  8.9 22.8 %collective-permute-start.5 = (f32[16,8,4,128]{3,0,2,1:T(8,128)S(1)}, f32[16,8,4,128]{3,0,2,1:T(8,128)S(1)}, u32[]{:S(2)}, u32[]{:S(2)}) collective-permute-start(f32[16,8,4,128]{3,0,2,1:T(8,128)S(1)} %copy.67), channel_id=1, source_target_pairs={{0,4},{4,8},{8,12},{1,5},{5,9},{9,13},{2,6},{6,10},{10,14},{3,7},{... | collective-permute-start | bytes 786440 | tf_op jit(solution)/shard_map/ppermute | solution.py:14
  14.0 18.5 %collective-permute-start = (f32[16,8,4,128]{3,0,2,1:T(8,128)S(1)}, f32[16,8,4,128]{3,0,2,1:T(8,128)S(1)}, u32[]{:S(2)}, u32[]{:S(2)}) collective-permute-start(f32[16,8,4,128]{3,0,2,1:T(8,128)S(1)} %copy.68), channel_id=1, source_target_pairs={{4,0},{8,4},{12,8},{5,1},{9,5},{13,9},{6,2},{10,6},{14,10},{7,3},{... | collective-permute-start | bytes 786440 | tf_op jit(solution)/shard_map/ppermute | solution.py:17
  15.5 6.9 %copy-start.1 = (f32[16,8,8,128]{3,2,1,0:T(8,128)S(1)}, f32[16,8,8,128]{3,2,1,0:T(8,128)}, u32[]{:S(2)}) copy-start(f32[16,8,8,128]{3,2,1,0:T(8,128)} %param.25) | copy-start | bytes 1572868
  15.5 10.2 %collective-permute-start.2 = (f32[6,8,3,128]{3,2,1,0:T(4,128)S(1)}, f32[6,8,3,128]{3,2,1,0:T(4,128)S(1)}, u32[]{:S(2)}, u32[]{:S(2)}) collective-permute-start(f32[6,8,3,128]{3,2,1,0:T(4,128)S(1)} %get-tuple-element.220), channel_id=1, source_target_pairs={{4,0},{8,4},{12,8},{5,1},{9,5},{13,9},{6,2},{10,6},{14,10},{7,3},{... | collective-permute-start | bytes 221192 | tf_op jit(solution)/shard_map/ppermute | solution.py:17
  17.0 8.8 %collective-permute-start.1 = (f32[6,8,3,128]{3,2,1,0:T(4,128)S(1)}, f32[6,8,3,128]{3,2,1,0:T(4,128)S(1)}, u32[]{:S(2)}, u32[]{:S(2)}) collective-permute-start(f32[6,8,3,128]{3,2,1,0:T(4,128)S(1)} %get-tuple-element.219), channel_id=1, source_target_pairs={{0,4},{4,8},{8,12},{1,5},{5,9},{9,13},{2,6},{6,10},{10,14},{3,7},{... | collective-permute-start | bytes 221192 | tf_op jit(solution)/shard_map/ppermute | solution.py:14
  25.8 4.4 %collective-permute-start.4 = (f32[6,3,14,128]{3,2,1,0:T(8,128)S(1)}, f32[6,3,14,128]{3,2,1,0:T(8,128)S(1)}, u32[]{:S(2)}, u32[]{:S(2)}) collective-permute-start(f32[6,3,14,128]{3,2,1,0:T(8,128)S(1)} %get-tuple-element.214), channel_id=1, source_target_pairs={{1,0},{3,2},{5,4},{7,6},{9,8},{11,10},{13,12},{15,14},{17,16},{19,... | collective-permute-start | bytes 387080 | tf_op jit(solution)/shard_map/ppermute | solution.py:17
  27.1 4.0 %collective-permute-start.3 = (f32[6,3,14,128]{3,2,1,0:T(8,128)S(1)}, f32[6,3,14,128]{3,2,1,0:T(8,128)S(1)}, u32[]{:S(2)}, u32[]{:S(2)}) collective-permute-start(f32[6,3,14,128]{3,2,1,0:T(8,128)S(1)} %get-tuple-element.213), channel_id=1, source_target_pairs={{0,1},{2,3},{4,5},{6,7},{8,9},{10,11},{12,13},{14,15},{16,17},{18,... | collective-permute-start | bytes 387080 | tf_op jit(solution)/shard_map/ppermute | solution.py:14
  32.6 4.8 %collective-permute-start.7 = (f32[16,4,16,128]{3,0,2,1:T(8,128)S(1)}, f32[16,4,16,128]{3,0,2,1:T(8,128)S(1)}, u32[]{:S(2)}, u32[]{:S(2)}) collective-permute-start(f32[16,4,16,128]{3,0,2,1:T(8,128)S(1)} %get-tuple-element.185), channel_id=1, source_target_pairs={{1,0},{3,2},{5,4},{7,6},{9,8},{11,10},{13,12},{15,14},{17,16},{19,... | collective-permute-start | bytes 1572872 | tf_op jit(solution)/shard_map/ppermute | solution.py:17
  33.9 4.6 %collective-permute-start.6 = (f32[16,4,16,128]{3,0,2,1:T(8,128)S(1)}, f32[16,4,16,128]{3,0,2,1:T(8,128)S(1)}, u32[]{:S(2)}, u32[]{:S(2)}) collective-permute-start(f32[16,4,16,128]{3,0,2,1:T(8,128)S(1)} %get-tuple-element.184), channel_id=1, source_target_pairs={{0,1},{2,3},{4,5},{6,7},{8,9},{10,11},{12,13},{14,15},{16,17},{18,... | collective-permute-start | bytes 1572872 | tf_op jit(solution)/shard_map/ppermute | solution.py:14
  55.4 11.2 %collective-permute-start.9 = (f32[19,12,2,128]{3,0,2,1:T(8,128)S(1)}, f32[19,12,2,128]{3,0,2,1:T(8,128)S(1)}, u32[]{:S(2)}, u32[]{:S(2)}) collective-permute-start(f32[19,12,2,128]{3,0,2,1:T(8,128)S(1)} %get-tuple-element.179), channel_id=1, source_target_pairs={{4,0},{8,4},{12,8},{5,1},{9,5},{13,9},{6,2},{10,6},{14,10},{7,3},{... | collective-permute-start | bytes 700424 | tf_op jit(solution)/shard_map/ppermute | solution.py:17
  56.7 11.1 %collective-permute-start.8 = (f32[19,12,2,128]{3,0,2,1:T(8,128)S(1)}, f32[19,12,2,128]{3,0,2,1:T(8,128)S(1)}, u32[]{:S(2)}, u32[]{:S(2)}) collective-permute-start(f32[19,12,2,128]{3,0,2,1:T(8,128)S(1)} %get-tuple-element.178), channel_id=1, source_target_pairs={{0,4},{4,8},{8,12},{1,5},{5,9},{9,13},{2,6},{6,10},{10,14},{3,7},{... | collective-permute-start | bytes 700424 | tf_op jit(solution)/shard_map/ppermute | solution.py:14
  67.8 2.7 %collective-permute-start.10 = (f32[19,2,16,128]{3,0,2,1:T(8,128)S(1)}, f32[19,2,16,128]{3,0,2,1:T(8,128)S(1)}, u32[]{:S(2)}, u32[]{:S(2)}) collective-permute-start(f32[19,2,16,128]{3,0,2,1:T(8,128)S(1)} %get-tuple-element.173), channel_id=1, source_target_pairs={{0,1},{2,3},{4,5},{6,7},{8,9},{10,11},{12,13},{14,15},{16,17},{18,... | collective-permute-start | bytes 933896 | tf_op jit(solution)/shard_map/ppermute | solution.py:14
  69.1 3.6 %collective-permute-start.11 = (f32[19,2,16,128]{3,0,2,1:T(8,128)S(1)}, f32[19,2,16,128]{3,0,2,1:T(8,128)S(1)}, u32[]{:S(2)}, u32[]{:S(2)}) collective-permute-start(f32[19,2,16,128]{3,0,2,1:T(8,128)S(1)} %get-tuple-element.172), channel_id=1, source_target_pairs={{1,0},{3,2},{5,4},{7,6},{9,8},{11,10},{13,12},{15,14},{17,16},{19,... | collective-permute-start | bytes 933896 | tf_op jit(solution)/shard_map/ppermute | solution.py:17
  82.6 11.7 %collective-permute-start.13 = (f32[19,12,2,128]{3,0,2,1:T(8,128)S(1)}, f32[19,12,2,128]{3,0,2,1:T(8,128)S(1)}, u32[]{:S(2)}, u32[]{:S(2)}) collective-permute-start(f32[19,12,2,128]{3,0,2,1:T(8,128)S(1)} %get-tuple-element.177), channel_id=1, source_target_pairs={{4,0},{8,4},{12,8},{5,1},{9,5},{13,9},{6,2},{10,6},{14,10},{7,3},{... | collective-permute-start | bytes 700424 | tf_op jit(solution)/shard_map/ppermute | solution.py:17
  83.9 11.6 %collective-permute-start.12 = (f32[19,12,2,128]{3,0,2,1:T(8,128)S(1)}, f32[19,12,2,128]{3,0,2,1:T(8,128)S(1)}, u32[]{:S(2)}, u32[]{:S(2)}) collective-permute-start(f32[19,12,2,128]{3,0,2,1:T(8,128)S(1)} %get-tuple-element.176), channel_id=1, source_target_pairs={{0,4},{4,8},{8,12},{1,5},{5,9},{9,13},{2,6},{6,10},{10,14},{3,7},{... | collective-permute-start | bytes 700424 | tf_op jit(solution)/shard_map/ppermute | solution.py:14
  95.5 2.7 %collective-permute-start.14 = (f32[19,2,16,128]{3,0,2,1:T(8,128)S(1)}, f32[19,2,16,128]{3,0,2,1:T(8,128)S(1)}, u32[]{:S(2)}, u32[]{:S(2)}) collective-permute-start(f32[19,2,16,128]{3,0,2,1:T(8,128)S(1)} %get-tuple-element.171), channel_id=1, source_target_pairs={{0,1},{2,3},{4,5},{6,7},{8,9},{10,11},{12,13},{14,15},{16,17},{18,... | collective-permute-start | bytes 933896 | tf_op jit(solution)/shard_map/ppermute | solution.py:14
  96.9 3.6 %collective-permute-start.15 = (f32[19,2,16,128]{3,0,2,1:T(8,128)S(1)}, f32[19,2,16,128]{3,0,2,1:T(8,128)S(1)}, u32[]{:S(2)}, u32[]{:S(2)}) collective-permute-start(f32[19,2,16,128]{3,0,2,1:T(8,128)S(1)} %get-tuple-element.170), channel_id=1, source_target_pairs={{1,0},{3,2},{5,4},{7,6},{9,8},{11,10},{13,12},{15,14},{17,16},{19,... | collective-permute-start | bytes 933896 | tf_op jit(solution)/shard_map/ppermute | solution.py:17
  98.3 3.1 %copy-start.8 = (u32[32]{0:T(128)S(1)}, u32[32]{0:T(128)}, u32[]{:S(2)}) copy-start(u32[32]{0:T(128)} %constant.419) | copy-start | bytes 388
Sparse Core Ops, SparseCore 0:
  101.5 23.3 all-reduce.88
where the time goes:
time: 134 us; the launch traced here: 133 us
  waiting for transfers between devices  42.6 us (32%)
  starting transfers between devices  39.2 us (29%)
  other arithmetic  26.9 us (20%)
  between operations  15.8 us (12%)
  local copies, waits for them, and re-layouts  8.55 us (6%)
    ppermute x8, starting transfers between devices, padded_2(): lax.ppermute(lax.slice_in_dim(block, block.shape[dim] - width, None, axis...  28.7 us
    unnamed x2, waiting for transfers between devices  21.3 us
    ppermute x8, waiting for transfers between devices, padded_2(): lax.ppermute(lax.slice_in_dim(block, 0, width, axis=dim), axis, backward)  17 us
    ppermute x8, starting transfers between devices, padded_2(): lax.ppermute(lax.slice_in_dim(block, 0, width, axis=dim), axis, backward)  10.5 us
    add_any x7, other arithmetic, face_flux(): rising = behind + 0.5 * albada(behind - far_behind, beyond - behind)  7.63 us
    unnamed x34, local copies, waits for them, and re-layouts  4.53 us
    ppermute x8, waiting for transfers between devices, padded_2(): lax.ppermute(lax.slice_in_dim(block, block.shape[dim] - width, None, axis...  4.34 us
    mul x3, other arithmetic, face_flux(): return opened * (velocity * carried - spread * (beyond - behind))  3.73 us
  transfers between devices with their start and end apart: 17, of which 10 were waited for; matrix products, arithmetic and copies ran while one was open for 4% of the time, Pallas kernels for 0%

commit v1 on v0

v1 whole, which is shorter than its diff:
```python
import functools

import jax
import jax.numpy as jnp
from jax import lax
from jax.experimental import pallas as pl
from jax.experimental.pallas import tpu as pltpu
from jax.sharding import PartitionSpec as P

ALBADA_FLOOR = 0.01
MESH = pl.DeviceIdType.MESH
ROWS = 8


def inverse(values):
    return pl.reciprocal(values, approx=True)


def limiter(lower, upper, lower_square, upper_square):
    half_inverse = inverse(lower_square + upper_square)
    product = lower * upper
    total = lower + upper
    return product * total * half_inverse, half_inverse, total


def doubled_square(step):
    return step * (step + step) + ALBADA_FLOOR


def forward_line(count, q, rise, fall, spread, emit):
    values = {x: q(x) for x in range(-2, count + 2)}
    steps = {c: values[c] - values[c - 1] for c in range(-1, count + 2)}
    squares = {c: doubled_square(steps[c]) for c in steps}
    through = {}
    above = None
    for x in range(-1, count + 1):
        slope, _, _ = limiter(steps[x], steps[x + 1], squares[x], squares[x + 1])
        if x >= 0:
            through[x] = (
                rise(x) * above + fall(x) * (values[x] - slope) - spread(x) * steps[x]
            )
        above = values[x] + slope
        if x >= 1:
            emit(x - 1, through[x - 1] - through[x])


def backward_line(count, q, g, rise, fall, spread, emit, speed):
    values = {x: q(x) for x in range(-2, count + 2)}
    steps = {c: values[c] - values[c - 1] for c in range(-1, count + 2)}
    squares = {c: doubled_square(steps[c]) for c in steps}
    cots = {x: g(x) for x in range(-2, count + 2)}
    up, down, jump, falls = {}, {}, {}, {}
    faces = {c: cots[c] - cots[c - 1] for c in range(-1, count + 2)}
    for c in range(0, count + 2):
        up[c] = faces[c] * rise(c)
    for c in range(-1, count + 1):
        falls[c] = fall(c)
        down[c] = faces[c] * falls[c]
    above, later = None, None
    for x in range(-1, count + 1):
        lower, upper = steps[x], steps[x + 1]
        slope, half_inverse, total = limiter(lower, upper, squares[x], squares[x + 1])
        weight = half_inverse * (up[x + 1] - down[x])
        fourfold = 4.0 * slope
        if x >= 0:
            first = (upper * (lower + total) - lower * fourfold) * weight
            jump[x] = first + later - spread(x) * faces[x]
        if x < count:
            later = (lower * (upper + total) - upper * fourfold) * weight
        if 0 <= x < count:
            carried = jnp.where(falls[x] < 0.0, values[x] - slope, above)
            speed(x, faces[x] * carried)
        above = values[x] + slope
        if x >= 1:
            emit(x - 1, (jump[x - 1] - jump[x]) + (up[x] + down[x - 1]))


def across(values, lane, last):
    before = jnp.where(lane == 0, 0.0, pltpu.roll(values, 1, 1))
    lower = values - before
    upper = jnp.where(lane == last, -values, pltpu.roll(lower, last, 1))
    return lower, upper


def forward_cell(values, rise, fall, spread, lane, last):
    lower, upper = across(values, lane, last)
    slope, _, _ = limiter(lower, upper, doubled_square(lower), doubled_square(upper))
    above = pltpu.roll(values + slope, 1, 1)
    through = rise * above + fall * (values - slope) - spread * lower
    return through - pltpu.roll(through, last, 1)


def backward_cell(values, cot, rise, fall, spread, lane, last):
    lower, upper = across(values, lane, last)
    slope, half_inverse, total = limiter(
        lower, upper, doubled_square(lower), doubled_square(upper)
    )
    face = cot - pltpu.roll(cot, 1, 1)
    up = pltpu.roll(face * rise, last, 1)
    down = face * fall
    weight = half_inverse * (up - down)
    fourfold = 4.0 * slope
    first = (upper * (lower + total) - lower * fourfold) * weight
    later = (lower * (upper + total) - upper * fourfold) * weight
    near = first - spread * face
    result = (
        near
        - later
        + up
        + down
        + jnp.where(lane == 0, 0.0, pltpu.roll(later, 1, 1))
        - jnp.where(lane == last, 0.0, pltpu.roll(near, last, 1))
    )
    carried = jnp.where(fall < 0.0, values - slope, pltpu.roll(values + slope, 1, 1))
    return result, face * carried


def kernel(
    sizes,
    dims,
    tracer_ref,
    cot_ref,
    zonal_ref,
    merid_ref,
    vert_ref,
    lateral_ref,
    vmix_ref,
    depth_ref,
    start_ref,
    speed_ref,
    first,
    last_cot,
    middle,
    middle_cot,
    pack,
    packed,
    vert_ext,
    vmix_ext,
    zonal_fields,
    vert_fields,
    merid_fields,
    opened_all,
    sums,
    reduced,
    arrived,
    halo_send,
    halo_recv,
    field_send,
    field_recv,
    sum_send,
    sum_recv,
):
    tiles, levs, groups_trc = sizes
    tracers, levels, columns, lanes = dims
    groups = tracers // ROWS
    end = lanes - 1
    cells = levels * columns
    tile, lev, trc = lax.axis_index("tile"), lax.axis_index("lev"), lax.axis_index("trc")
    lane = lax.broadcasted_iota(jnp.int32, (ROWS, lanes), 1)

    below = {"tile": tile > 0, "lev": lev > 0}
    beyond = {"tile": tile < tiles - 1, "lev": lev < levs - 1}
    place = {"tile": tile, "lev": lev}
    size = {"tile": tiles, "lev": levs}
    axes = [axis for axis in ("tile", "lev") if size[axis] > 1]

    barrier = pltpu.get_barrier_semaphore()
    expected = groups_trc - 1
    for axis in axes:
        for there, offset in ((below[axis], -1), (beyond[axis], 1)):

            @pl.when(there)
            def _(axis=axis, offset=offset):
                pl.semaphore_signal(
                    barrier,
                    inc=1,
                    device_id={axis: place[axis] + offset},
                    device_id_type=MESH,
                )

            expected = expected + there.astype(jnp.int32)
    for step in range(1, groups_trc):
        pl.semaphore_signal(
            barrier,
            inc=1,
            device_id={"trc": lax.rem(trc + step, groups_trc)},
            device_id_type=MESH,
        )

    def wet(level):
        known = jnp.logical_and(level < depth_ref[...], level >= 0)
        return jnp.where(known, 1.0, 0.0)

    def load_own(l, carry):
        for g in range(groups):
            for i in range(columns):
                rows = pl.ds(g * ROWS * cells + l * columns + i, ROWS, stride=cells)
                first[g, l + 2, i + 2] = tracer_ref[rows, :]
                last_cot[g, l + 2, i + 2] = cot_ref[rows, :]
        here = wet(lev * levels + l)
        zonal, lateral = zonal_ref[l], lateral_ref[l]
        for side, rows in ((0, slice(0, 2)), (1, slice(columns - 2, columns))):
            pack[side, l] = jnp.concatenate(
                [zonal[rows], lateral[rows], here[rows], here[rows]], axis=0
            )
        vert_ext[l + 2] = vert_ref[l]
        vmix_ext[l + 2] = vmix_ref[l]
        return carry

    lax.fori_loop(0, levels, load_own, 0)

    zero_tile = jnp.zeros((ROWS, lanes), jnp.float32)

    def clear(side):
        for buffer in (first, last_cot, middle, middle_cot):
            for g in range(groups):
                if side < 2:
                    place_at = columns + 2 if side == 0 else 0

                    def clear_row(l, carry):
                        buffer[g, l + 2, place_at] = zero_tile
                        buffer[g, l + 2, place_at + 1] = zero_tile
                        return carry

                    lax.fori_loop(0, levels, clear_row, 0)
                else:
                    place_at = levels + 2 if side == 2 else 0

                    def clear_column(i, carry):
                        buffer[g, place_at, i + 2] = zero_tile
                        buffer[g, place_at + 1, i + 2] = zero_tile
                        return carry

                    lax.fori_loop(0, columns, clear_column, 0)
        if side < 2:
            packed[side] = jnp.zeros_like(packed[side])
        else:
            place_at = levels + 2 if side == 2 else 0
            for buffer in (vert_ext, vmix_ext):
                buffer[place_at] = zero_tile_rows
                buffer[place_at + 1] = zero_tile_rows

    zero_tile_rows = jnp.zeros((columns, lanes), jnp.float32)
    for side, axis, there in (
        (0, "tile", beyond["tile"]),
        (1, "tile", below["tile"]),
        (2, "lev", beyond["lev"]),
        (3, "lev", below["lev"]),
    ):
        if size[axis] > 1:

            @pl.when(jnp.logical_not(there))
            def _(side=side):
                clear(side)

        else:
            clear(side)

    pl.semaphore_wait(barrier, expected)

    def exchange(pairs, send_sem, recv_sem):
        copies = []
        for side, source, destination in pairs:
            axis = "tile" if side in (0, 1) else "lev"
            if size[axis] == 1:
                continue
            goes_down = side in (0, 2)
            copy = pltpu.make_async_remote_copy(
                src_ref=source,
                dst_ref=destination,
                send_sem=send_sem(side),
                recv_sem=recv_sem(side),
                device_id={axis: place[axis] + (-1 if goes_down else 1)},
                device_id_type=MESH,
            )
            sends = below[axis] if goes_down else beyond[axis]
            receives = beyond[axis] if goes_down else below[axis]
            copies.append((copy, sends, receives))
        return copies

    def start(copies):
        for copy, sends, _ in copies:
            pl.when(sends)(copy.start)

    def arrive(copies):
        for copy, _, receives in copies:
            pl.when(receives)(copy.wait_recv)

    def finish(copies):
        for copy, sends, _ in copies:
            pl.when(sends)(copy.wait_send)

    own_l, own_i = pl.ds(2, levels), pl.ds(2, columns)

    def halo(buffer, stage, g):
        pairs = [
            (0, buffer.at[g, own_l, pl.ds(2, 2)], buffer.at[g, own_l, pl.ds(columns + 2, 2)]),
            (1, buffer.at[g, own_l, pl.ds(columns, 2)], buffer.at[g, own_l, pl.ds(0, 2)]),
            (2, buffer.at[g, pl.ds(2, 2), own_i], buffer.at[g, pl.ds(levels + 2, 2), own_i]),
            (3, buffer.at[g, pl.ds(levels, 2), own_i], buffer.at[g, pl.ds(0, 2), own_i]),
        ]
        return exchange(
            pairs,
            lambda side: halo_send.at[stage, g, side],
            lambda side: halo_recv.at[stage, g, side],
        )

    field_copies = exchange(
        [(0, pack.at[0], packed.at[0]), (1, pack.at[1], packed.at[1])],
        lambda side: field_send.at[0, side],
        lambda side: field_recv.at[0, side],
    )
    for row, buffer in enumerate((vert_ext, vmix_ext)):
        field_copies += exchange(
            [
                (2, buffer.at[pl.ds(2, 2)], buffer.at[pl.ds(levels + 2, 2)]),
                (3, buffer.at[pl.ds(levels, 2)], buffer.at[pl.ds(0, 2)]),
            ],
            lambda side, row=row: field_send.at[row, side],
            lambda side, row=row: field_recv.at[row, side],
        )
    first_copies = [halo(first, 0, g) for g in range(groups)]
    cot_copies = [halo(last_cot, 1, g) for g in range(groups)]
    middle_copies = [halo(middle, 2, g) for g in range(groups)]
    back_copies = [halo(middle_cot, 3, g) for g in range(groups)]

    start(field_copies)
    for copies in first_copies + cot_copies:
        start(copies)

    def spread_rows(target, head, opened, speed, mixing, count):
        kinds = (
            opened * jnp.maximum(speed, 0.0),
            opened * jnp.minimum(speed, 0.0),
            opened * mixing,
        )
        for kind, values in enumerate(kinds):
            for i in range(count):
                target[(kind,) + head + (i,)] = jnp.broadcast_to(
                    values[i : i + 1], (ROWS, lanes)
                )

    def merid_build(l, carry):
        here = wet(lev * levels + l)
        south = jnp.where(lane[:columns] == 0, 0.0, pltpu.roll(here, 1, 1))
        opened = here * south
        opened_all[1, l] = opened
        spread_rows(merid_fields, (l,), opened, merid_ref[l], lateral_ref[l], columns)
        return carry

    lax.fori_loop(0, levels, merid_build, 0)

    def forward_merid(g):
        def step(l, carry):
            for i in range(columns):
                values = first[g, l + 2, i + 2]
                middle[g, l + 2, i + 2] = values + forward_cell(
                    values,
                    merid_fields[0, l, i],
                    merid_fields[1, l, i],
                    merid_fields[2, l, i],
                    lane,
                    end,
                )
            return carry

        lax.fori_loop(0, levels, step, 0)

    for g in range(groups):
        forward_merid(g)

    arrive(field_copies)

    def zonal_build(l, carry):
        low, high = packed[1, l], packed[0, l]
        here = wet(lev * levels + l)
        wets = jnp.concatenate([low[4:6], here, high[4:6]], axis=0)
        speed = jnp.concatenate([low[1:2], zonal_ref[l], high[0:2]], axis=0)
        mixing = jnp.concatenate([low[3:4], lateral_ref[l], high[2:4]], axis=0)
        opened = wets[:-1] * wets[1:]
        opened_all[0, l] = opened[1 : columns + 1]
        spread_rows(zonal_fields, (l,), opened, speed, mixing, columns + 3)
        return carry

    lax.fori_loop(0, levels, zonal_build, 0)

    def vert_build(row, carry):
        level = lev * levels + row - 1
        opened = wet(level - 1) * wet(level)
        spread_rows(
            vert_fields, (row,), opened, vert_ext[row + 1], vmix_ext[row + 1], columns
        )
        return carry

    lax.fori_loop(0, levels + 3, vert_build, 0)

    def vert_opened(l, carry):
        level = lev * levels + l
        opened_all[2, l] = wet(level - 1) * wet(level)
        return carry

    lax.fori_loop(0, levels, vert_opened, 0)

    def forward_zonal(g):
        def step(l, carry):
            def emit(x, value):
                middle[g, l + 2, x + 2] += value

            forward_line(
                columns,
                lambda x: first[g, l + 2, x + 2],
                lambda c: zonal_fields[0, l, c + 1],
                lambda c: zonal_fields[1, l, c + 1],
                lambda c: zonal_fields[2, l, c + 1],
                emit,
            )
            return carry

        lax.fori_loop(0, levels, step, 0)

    def forward_vert(g):
        def step(i, carry):
            def emit(x, value):
                middle[g, x + 2, i + 2] += value

            forward_line(
                levels,
                lambda x: first[g, x + 2, i + 2],
                lambda c: vert_fields[0, c + 1, i],
                lambda c: vert_fields[1, c + 1, i],
                lambda c: vert_fields[2, c + 1, i],
                emit,
            )
            return carry

        lax.fori_loop(0, columns, step, 0)

    def pull_merid(state, cot, store, g, fresh):
        def step(l, carry):
            for i in range(columns):
                own_cot = cot[g, l + 2, i + 2]
                pulled, share = backward_cell(
                    state[g, l + 2, i + 2],
                    own_cot,
                    merid_fields[0, l, i],
                    merid_fields[1, l, i],
                    merid_fields[2, l, i],
                    lane,
                    end,
                )
                store(g, l, i, own_cot + pulled, True)
                sums[1, l, i] = share if fresh else sums[1, l, i] + share
            return carry

        lax.fori_loop(0, levels, step, 0)

    def pull_zonal(state, cot, store, g, fresh):
        def step(l, carry):
            def speed(c, value):
                sums[0, l, c] = value if fresh else sums[0, l, c] + value

            backward_line(
                columns,
                lambda x: state[g, l + 2, x + 2],
                lambda x: cot[g, l + 2, x + 2],
                lambda c: zonal_fields[0, l, c + 1],
                lambda c: zonal_fields[1, l, c + 1],
                lambda c: zonal_fields[2, l, c + 1],
                lambda x, value: store(g, l, x, value, False),
                speed,
            )
            return carry

        lax.fori_loop(0, levels, step, 0)

    def pull_vert(state, cot, store, g, fresh):
        def step(i, carry):
            def speed(c, value):
                sums[2, c, i] = value if fresh else sums[2, c, i] + value

            backward_line(
                levels,
                lambda x: state[g, x + 2, i + 2],
                lambda x: cot[g, x + 2, i + 2],
                lambda c: vert_fields[0, c + 1, i],
                lambda c: vert_fields[1, c + 1, i],
                lambda c: vert_fields[2, c + 1, i],
                lambda x, value: store(g, x, i, value, False),
                speed,
            )
            return carry

        lax.fori_loop(0, columns, step, 0)

    def store_middle(g, l, i, value, fresh):
        if fresh:
            middle_cot[g, l + 2, i + 2] = value
        else:
            middle_cot[g, l + 2, i + 2] += value

    def store_start(g, l, i, value, fresh):
        rows = pl.ds(g * ROWS * cells + l * columns + i, ROWS, stride=cells)
        if fresh:
            start_ref[rows, :] = value
        else:
            start_ref[rows, :] = start_ref[rows, :] + value

    for g in range(groups):
        arrive(first_copies[g])
        forward_zonal(g)
        forward_vert(g)
        start(middle_copies[g])
    for g in range(groups):
        pull_merid(middle, last_cot, store_middle, g, g == 0)
    for g in range(groups):
        arrive(cot_copies[g])
        arrive(middle_copies[g])
        pull_zonal(middle, last_cot, store_middle, g, g == 0)
        pull_vert(middle, last_cot, store_middle, g, g == 0)
        start(back_copies[g])
    for g in range(groups):
        pull_merid(first, middle_cot, store_start, g, False)
    for g in range(groups):
        arrive(back_copies[g])
        pull_zonal(first, middle_cot, store_start, g, False)
        pull_vert(first, middle_cot, store_start, g, False)

    def reduce_level(l, carry):
        for row in range(3):
            reduced[row, l] = opened_all[row, l] * jnp.sum(sums[row, l], axis=1)
        return carry

    lax.fori_loop(0, levels, reduce_level, 0)
    share = levels // groups_trc
    sum_copies = []
    for step in range(1, groups_trc):
        target = lax.rem(trc + step, groups_trc)
        copy = pltpu.make_async_remote_copy(
            src_ref=reduced.at[:, pl.ds(target * share, share)],
            dst_ref=arrived.at[step - 1],
            send_sem=sum_send.at[step - 1],
            recv_sem=sum_recv.at[step - 1],
            device_id={"trc": target},
            device_id_type=MESH,
        )
        copy.start()
        sum_copies.append(copy)
    total = reduced[:, pl.ds(trc * share, share)]
    for step, copy in enumerate(sum_copies):
        copy.wait_recv()
        total = total + arrived[step]
    speed_ref[...] = total

    for copies in [field_copies] + first_copies + cot_copies + middle_copies + back_copies:
        finish(copies)
    for copy in sum_copies:
        copy.wait_send()


def body(sizes, tracers, cotangent, *fields):
    count, levels, columns, lanes = tracers.shape
    groups = count // ROWS
    share = levels // sizes[2]
    extended = pltpu.VMEM((groups, levels + 4, columns + 4, ROWS, lanes), jnp.float32)
    flat = (count * levels * columns, lanes)
    start_cot, speed_cot = pl.pallas_call(
        functools.partial(kernel, sizes, tracers.shape),
        out_shape=(
            jax.ShapeDtypeStruct(flat, jnp.float32),
            jax.ShapeDtypeStruct((3, share, columns, lanes), jnp.float32),
        ),
        in_specs=[pl.BlockSpec(memory_space=pltpu.VMEM)] * 8,
        out_specs=(pl.BlockSpec(memory_space=pltpu.VMEM),) * 2,
        scratch_shapes=[
            extended,
            extended,
            extended,
            extended,
            pltpu.VMEM((2, levels, 8, lanes), jnp.float32),
            pltpu.VMEM((2, levels, 8, lanes), jnp.float32),
            pltpu.VMEM((levels + 4, columns, lanes), jnp.float32),
            pltpu.VMEM((levels + 4, columns, lanes), jnp.float32),
            pltpu.VMEM((3, levels, columns + 3, ROWS, lanes), jnp.float32),
            pltpu.VMEM((3, levels + 3, columns, ROWS, lanes), jnp.float32),
            pltpu.VMEM((3, levels, columns, ROWS, lanes), jnp.float32),
            pltpu.VMEM((3, levels, columns, lanes), jnp.float32),
            pltpu.VMEM((3, levels, columns, ROWS, lanes), jnp.float32),
            pltpu.VMEM((3, levels, columns, lanes), jnp.float32),
            pltpu.VMEM((max(sizes[2] - 1, 1), 3, share, columns, lanes), jnp.float32),
            pltpu.SemaphoreType.DMA((4, groups, 4)),
            pltpu.SemaphoreType.DMA((4, groups, 4)),
            pltpu.SemaphoreType.DMA((2, 4)),
            pltpu.SemaphoreType.DMA((2, 4)),
            pltpu.SemaphoreType.DMA((max(sizes[2] - 1, 1),)),
            pltpu.SemaphoreType.DMA((max(sizes[2] - 1, 1),)),
        ],
        compiler_params=pltpu.CompilerParams(
            collective_id=0, has_side_effects=True, vmem_limit_bytes=48 * 1024 * 1024
        ),
    )(tracers.reshape(flat), cotangent.reshape(flat), *fields)
    return start_cot.reshape(tracers.shape), speed_cot


def solution(mesh):
    sizes = (mesh.shape["tile"], mesh.shape["lev"], mesh.shape["trc"])
    return jax.shard_map(
        functools.partial(body, sizes),
        mesh=mesh,
        in_specs=(
            P("trc", "lev", ("ens", "tile"), None),
            P("trc", "lev", ("ens", "tile"), None),
            P("lev", ("ens", "tile"), None),
            P("lev", ("ens", "tile"), None),
            P("lev", ("ens", "tile"), None),
            P("lev", ("ens", "tile"), None),
            P("lev", ("ens", "tile"), None),
            P(("ens", "tile"), None),
        ),
        out_specs=(
            P("trc", "lev", ("ens", "tile"), None),
            P(None, ("lev", "trc"), ("ens", "tile"), None),
        ),
        check_vma=False,
    )
```

time: 134 us -> 36.6 us (0.27)
  waiting for transfers between devices: 42.6 us -> 0 us
  starting transfers between devices: 39.2 us -> 0 us
  Pallas kernels: 0 us -> 27.4 us
  other arithmetic: 26.9 us -> 0 us
  between operations: 15.8 us -> 0.66 us
    ppermute x16 -> x0, starting transfers between devices: 39.1 us -> none  [the longest x8 28.7 us: padded_2(): lax.ppermute(lax.slice_in_dim(block, block.shape[dim] - width, None, axis...]
    pallas_call x0 -> x1, Pallas kernels: none -> 27.4 us  [body(): pl.pallas_call(functools.partial(kernel, sizes, tracers.shape), out_shape...]
    ppermute x16 -> x0, waiting for transfers between devices: 21.4 us -> none  [the longest x8 17 us: padded_2(): lax.ppermute(lax.slice_in_dim(block, 0, width, axis=dim), axis, backward)]
    unnamed x2 -> x0, waiting for transfers between devices: 21.3 us -> none
    add_any x19 -> x0, other arithmetic: 13.1 us -> none  [the longest x7 7.63 us: face_flux(): rising = behind + 0.5 * albada(behind - far_behind, beyond - behind)]
    mul x15 -> x0, other arithmetic: 4.18 us -> none  [the longest x3 3.73 us: face_flux(): return opened * (velocity * carried - spread * (beyond - behind))]
    reduce_sum x6 -> x0, other arithmetic: 3.6 us -> none  [face_flux(): return opened * (velocity * carried - spread * (beyond - behind))]
    unnamed x34 -> x18, local copies, waits for them, and re-layouts: 4.53 us -> 7.96 us
  transfers between devices with their start and end apart: 17 -> 0, of which waited for: 10 -> 0; matrix products, arithmetic and copies ran while one was open for 4% -> 0% of each run, Pallas kernels for 0% -> 0%
where the time goes in v1:
time: 36.6 us; the launch traced here: 36 us
  Pallas kernels  27.4 us (75%)
  local copies, waits for them, and re-layouts  7.96 us (22%)
  between operations  0.66 us (2%)
    pallas_call x1, Pallas kernels, body(): pl.pallas_call(functools.partial(kernel, sizes, tracers.shape), out_shape...  27.4 us
    unnamed x18, local copies, waits for them, and re-layouts  7.96 us

profile of v1, /device:TPU:0, one launch (start us, length us, event | category | flops | bytes accessed | tf_op | source)
XLA Modules:
  0.0 36.0 jit_solution(2453861499449365670)
XLA Ops:
  0.6 0.0 copy-start
  0.6 1.0 %copy-done = f32[16,8,8,128]{3,2,1,0:T(8,128)S(1)} copy-done((f32[16,8,8,128]{3,2,1,0:T(8,128)S(1)}, f32[16,8,8,128]{3,2,1,0:T(8,128)}, u32[]{:S(2)}) %copy-start) | copy-done | bytes 524312
  1.7 0.0 copy-start.1
  1.7 1.0 %copy-done.1 = f32[16,8,8,128]{3,2,1,0:T(8,128)S(1)} copy-done((f32[16,8,8,128]{3,2,1,0:T(8,128)S(1)}, f32[16,8,8,128]{3,2,1,0:T(8,128)}, u32[]{:S(2)}) %copy-start.1) | copy-done | bytes 524312
  2.7 0.0 copy-start.2
  2.7 0.8 %copy-done.2 = f32[8,8,128]{2,1,0:T(8,128)S(1)} copy-done((f32[8,8,128]{2,1,0:T(8,128)S(1)}, f32[8,8,128]{2,1,0:T(8,128)}, u32[]{:S(2)}) %copy-start.2) | copy-done | bytes 32792
  3.5 0.0 copy-start.3
  3.5 0.8 %copy-done.3 = f32[8,8,128]{2,1,0:T(8,128)S(1)} copy-done((f32[8,8,128]{2,1,0:T(8,128)S(1)}, f32[8,8,128]{2,1,0:T(8,128)}, u32[]{:S(2)}) %copy-start.3) | copy-done | bytes 32792
  4.2 0.0 copy-start.4
  4.2 0.8 %copy-done.4 = f32[8,8,128]{2,1,0:T(8,128)S(1)} copy-done((f32[8,8,128]{2,1,0:T(8,128)S(1)}, f32[8,8,128]{2,1,0:T(8,128)}, u32[]{:S(2)}) %copy-start.4) | copy-done | bytes 32792
  5.0 0.0 copy-start.5
  5.0 0.8 %copy-done.5 = f32[8,8,128]{2,1,0:T(8,128)S(1)} copy-done((f32[8,8,128]{2,1,0:T(8,128)S(1)}, f32[8,8,128]{2,1,0:T(8,128)}, u32[]{:S(2)}) %copy-start.5) | copy-done | bytes 32792
  5.8 0.0 copy-start.6
  5.8 0.8 %copy-done.6 = f32[8,8,128]{2,1,0:T(8,128)S(1)} copy-done((f32[8,8,128]{2,1,0:T(8,128)S(1)}, f32[8,8,128]{2,1,0:T(8,128)}, u32[]{:S(2)}) %copy-start.6) | copy-done | bytes 32792
  6.5 0.0 copy-start.7
  6.5 0.7 %copy-done.7 = s32[8,128]{1,0:T(8,128)S(1)} copy-done((s32[8,128]{1,0:T(8,128)S(1)}, s32[8,128]{1,0:T(8,128)}, u32[]{:S(2)}) %copy-start.7) | copy-done | bytes 4120
  7.2 27.4 %shard_map.95 = (f32[1024,128]{1,0:T(8,128)S(1)}, f32[3,4,8,128]{3,2,1,0:T(8,128)S(1)}) custom-call(f32[1024,128]{1,0:T(8,128)S(1)} %bitcast.3, f32[1024,128]{1,0:T(8,128)S(1)} %bitcast.4, f32[8,8,128]{2,1,0:T(8,128)S(1)} %copy-done.2, f32[8,8,128]{2,1,0:T(8,128)S(1)} %copy-done.3, f32[8,8,128]{2,1,0:T(8,128)S(1)} %copy-done.4, f32[8,8,128]{2,1,0:T(8,128)S(1)} %copy-done.5, ...), custom_call_target="tpu_custom_call" | custom-call | tf_op jit(solution)/shard_map/pallas_call | solution.py:566
  34.6 0.8 %copy.12 = f32[16,8,8,128]{3,2,1,0:T(8,128)} copy(f32[16,8,8,128]{3,2,1,0:T(8,128)S(1)} %bitcast.5) | data formatting | bytes 1048576
  35.4 0.6 %copy.13 = f32[3,4,8,128]{3,2,1,0:T(8,128)} copy(f32[3,4,8,128]{3,2,1,0:T(8,128)S(1)} %get-tuple-element.9) | data formatting | bytes 98304
Async XLA Ops:
  0.6 1.0 %copy-start = (f32[16,8,8,128]{3,2,1,0:T(8,128)S(1)}, f32[16,8,8,128]{3,2,1,0:T(8,128)}, u32[]{:S(2)}) copy-start(f32[16,8,8,128]{3,2,1,0:T(8,128)} %param.8) | copy-start | bytes 1572868
  1.7 1.0 %copy-start.1 = (f32[16,8,8,128]{3,2,1,0:T(8,128)S(1)}, f32[16,8,8,128]{3,2,1,0:T(8,128)}, u32[]{:S(2)}) copy-start(f32[16,8,8,128]{3,2,1,0:T(8,128)} %param.9) | copy-start | bytes 1572868
  2.7 0.8 %copy-start.2 = (f32[8,8,128]{2,1,0:T(8,128)S(1)}, f32[8,8,128]{2,1,0:T(8,128)}, u32[]{:S(2)}) copy-start(f32[8,8,128]{2,1,0:T(8,128)} %zonal_ref.1) | copy-start | bytes 98308
  3.5 0.8 %copy-start.3 = (f32[8,8,128]{2,1,0:T(8,128)S(1)}, f32[8,8,128]{2,1,0:T(8,128)}, u32[]{:S(2)}) copy-start(f32[8,8,128]{2,1,0:T(8,128)} %merid_ref.1) | copy-start | bytes 98308
  4.2 0.8 %copy-start.4 = (f32[8,8,128]{2,1,0:T(8,128)S(1)}, f32[8,8,128]{2,1,0:T(8,128)}, u32[]{:S(2)}) copy-start(f32[8,8,128]{2,1,0:T(8,128)} %vert_ref.1) | copy-start | bytes 98308
  5.0 0.8 %copy-start.5 = (f32[8,8,128]{2,1,0:T(8,128)S(1)}, f32[8,8,128]{2,1,0:T(8,128)}, u32[]{:S(2)}) copy-start(f32[8,8,128]{2,1,0:T(8,128)} %lateral_ref.1) | copy-start | bytes 98308
  5.8 0.8 %copy-start.6 = (f32[8,8,128]{2,1,0:T(8,128)S(1)}, f32[8,8,128]{2,1,0:T(8,128)}, u32[]{:S(2)}) copy-start(f32[8,8,128]{2,1,0:T(8,128)} %vmix_ref.1) | copy-start | bytes 98308
  6.5 0.7 %copy-start.7 = (s32[8,128]{1,0:T(8,128)S(1)}, s32[8,128]{1,0:T(8,128)}, u32[]{:S(2)}) copy-start(s32[8,128]{1,0:T(8,128)} %depth_ref.1) | copy-start | bytes 12292

commit v2 on v1

--- a/solution.py
+++ b/solution.py
@@ -118,14 +118,14 @@
 def kernel(
     sizes,
     dims,
-    tracer_ref,
-    cot_ref,
-    zonal_ref,
-    merid_ref,
-    vert_ref,
-    lateral_ref,
-    vmix_ref,
-    depth_ref,
+    tracer_hbm,
+    cot_hbm,
+    zonal_hbm,
+    merid_hbm,
+    vert_hbm,
+    lateral_hbm,
+    vmix_hbm,
+    depth_hbm,
     start_ref,
     speed_ref,
     first,
@@ -149,7 +149,36 @@
     field_recv,
     sum_send,
     sum_recv,
+    start_sum,
+    load_sem,
+    *loaded,
 ):
+    outside = (
+        tracer_hbm,
+        cot_hbm,
+        zonal_hbm,
+        merid_hbm,
+        vert_hbm,
+        lateral_hbm,
+        vmix_hbm,
+        depth_hbm,
+    )
+    loads = [
+        pltpu.make_async_copy(source, target, load_sem.at[row])
+        for row, (source, target) in enumerate(zip(outside, loaded))
+    ]
+    for load in loads:
+        load.start()
+    (
+        tracer_ref,
+        cot_ref,
+        zonal_ref,
+        merid_ref,
+        vert_ref,
+        lateral_ref,
+        vmix_ref,
+        depth_ref,
+    ) = loaded
     tiles, levs, groups_trc = sizes
     tracers, levels, columns, lanes = dims
     groups = tracers // ROWS
@@ -207,8 +236,6 @@
         vmix_ext[l + 2] = vmix_ref[l]
         return carry
 
-    lax.fori_loop(0, levels, load_own, 0)
-
     zero_tile = jnp.zeros((ROWS, lanes), jnp.float32)
 
     def clear(side):
@@ -255,6 +282,10 @@
 
         else:
             clear(side)
+
+    for load in loads:
+        load.wait()
+    lax.fori_loop(0, levels, load_own, 0)
 
     pl.semaphore_wait(barrier, expected)
 
@@ -275,19 +306,20 @@
             )
             sends = below[axis] if goes_down else beyond[axis]
             receives = beyond[axis] if goes_down else below[axis]
-            copies.append((copy, sends, receives))
+            copies.append((copy, sends, receives, axis))
         return copies
 
     def start(copies):
-        for copy, sends, _ in copies:
+        for copy, sends, _, _ in copies:
             pl.when(sends)(copy.start)
 
-    def arrive(copies):
-        for copy, _, receives in copies:
-            pl.when(receives)(copy.wait_recv)
+    def arrive(copies, along=("tile", "lev")):
+        for copy, _, receives, axis in copies:
+            if axis in along:
+                pl.when(receives)(copy.wait_recv)
 
     def finish(copies):
-        for copy, sends, _ in copies:
+        for copy, sends, _, _ in copies:
             pl.when(sends)(copy.wait_send)
 
     own_l, own_i = pl.ds(2, levels), pl.ds(2, columns)
@@ -324,8 +356,9 @@
     middle_copies = [halo(middle, 2, g) for g in range(groups)]
     back_copies = [halo(middle_cot, 3, g) for g in range(groups)]
 
+    start(first_copies[0])
     start(field_copies)
-    for copies in first_copies + cot_copies:
+    for copies in first_copies[1:] + cot_copies:
         start(copies)
 
     def spread_rows(target, head, opened, speed, mixing, count):
@@ -369,8 +402,6 @@
     for g in range(groups):
         forward_merid(g)
 
-    arrive(field_copies)
-
     def zonal_build(l, carry):
         low, high = packed[1, l], packed[0, l]
         here = wet(lev * levels + l)
@@ -382,8 +413,6 @@
         spread_rows(zonal_fields, (l,), opened, speed, mixing, columns + 3)
         return carry
 
-    lax.fori_loop(0, levels, zonal_build, 0)
-
     def vert_build(row, carry):
         level = lev * levels + row - 1
         opened = wet(level - 1) * wet(level)
@@ -392,14 +421,10 @@
         )
         return carry
 
-    lax.fori_loop(0, levels + 3, vert_build, 0)
-
     def vert_opened(l, carry):
         level = lev * levels + l
         opened_all[2, l] = wet(level - 1) * wet(level)
         return carry
-
-    lax.fori_loop(0, levels, vert_opened, 0)
 
     def forward_zonal(g):
         def step(l, carry):
@@ -454,8 +479,10 @@
 
         lax.fori_loop(0, levels, step, 0)
 
-    def pull_zonal(state, cot, store, g, fresh):
-        def step(l, carry):
+    def pull_zonal(state, cot, store, g, fresh, begin=0, count=levels):
+        def step(index, carry):
+            l = lax.rem(begin + index, levels)
+
             def speed(c, value):
                 sums[0, l, c] = value if fresh else sums[0, l, c] + value
 
@@ -471,7 +498,7 @@
             )
             return carry
 
-        lax.fori_loop(0, levels, step, 0)
+        lax.fori_loop(0, count, step, 0)
 
     def pull_vert(state, cot, store, g, fresh):
         def step(i, carry):
@@ -499,56 +526,85 @@
             middle_cot[g, l + 2, i + 2] += value
 
     def store_start(g, l, i, value, fresh):
+        if fresh:
+            start_sum[g, l, i] = value
+        else:
+            start_sum[g, l, i] += value
+
+    def store_last(g, l, i, value, fresh):
         rows = pl.ds(g * ROWS * cells + l * columns + i, ROWS, stride=cells)
-        if fresh:
-            start_ref[rows, :] = value
-        else:
-            start_ref[rows, :] = start_ref[rows, :] + value
-
-    for g in range(groups):
-        arrive(first_copies[g])
+        start_ref[rows, :] = start_sum[g, l, i] + value
+
+    for g in range(groups):
+        arrive(first_copies[g], ("lev",))
+        if g == 0:
+            arrive(field_copies)
+            lax.fori_loop(0, levels, zonal_build, 0)
+            lax.fori_loop(0, levels + 3, vert_build, 0)
+            lax.fori_loop(0, levels, vert_opened, 0)
+        forward_vert(g)
+        arrive(first_copies[g], ("tile",))
         forward_zonal(g)
-        forward_vert(g)
         start(middle_copies[g])
     for g in range(groups):
         pull_merid(middle, last_cot, store_middle, g, g == 0)
     for g in range(groups):
         arrive(cot_copies[g])
-        arrive(middle_copies[g])
+        arrive(middle_copies[g], ("lev",))
+        pull_vert(middle, last_cot, store_middle, g, g == 0)
+        arrive(middle_copies[g], ("tile",))
         pull_zonal(middle, last_cot, store_middle, g, g == 0)
-        pull_vert(middle, last_cot, store_middle, g, g == 0)
         start(back_copies[g])
     for g in range(groups):
         pull_merid(first, middle_cot, store_start, g, False)
     for g in range(groups):
-        arrive(back_copies[g])
-        pull_zonal(first, middle_cot, store_start, g, False)
+        arrive(back_copies[g], ("lev",))
         pull_vert(first, middle_cot, store_start, g, False)
 
-    def reduce_level(l, carry):
-        for row in range(3):
-            reduced[row, l] = opened_all[row, l] * jnp.sum(sums[row, l], axis=1)
-        return carry
-
-    lax.fori_loop(0, levels, reduce_level, 0)
     share = levels // groups_trc
     sum_copies = []
+
+    def reduce_rows(rows, begin, count):
+        def step(index, carry):
+            l = lax.rem(begin + index, levels)
+            for row in rows:
+                reduced[row, l] = opened_all[row, l] * jnp.sum(sums[row, l], axis=1)
+            return carry
+
+        lax.fori_loop(0, count, step, 0)
+
+    def send_rows(part, rows):
+        for step in range(1, groups_trc):
+            target = lax.rem(trc + step, groups_trc)
+            copy = pltpu.make_async_remote_copy(
+                src_ref=reduced.at[rows, pl.ds(target * share, share)],
+                dst_ref=arrived.at[step - 1, rows],
+                send_sem=sum_send.at[part, step - 1],
+                recv_sem=sum_recv.at[part, step - 1],
+                device_id={"trc": target},
+                device_id_type=MESH,
+            )
+            copy.start()
+            sum_copies.append(copy)
+
+    reduce_rows((1, 2), 0, levels)
+    send_rows(0, pl.ds(1, 2))
+    for g in range(groups):
+        arrive(back_copies[g], ("tile",))
+    after = (trc + 1) * share
+    if groups_trc > 1:
+        for g in range(groups):
+            pull_zonal(first, middle_cot, store_last, g, False, after, levels - share)
+        reduce_rows((0,), after, levels - share)
+        send_rows(1, pl.ds(0, 1))
+    for g in range(groups):
+        pull_zonal(first, middle_cot, store_last, g, False, trc * share, share)
+    reduce_rows((0,), trc * share, share)
+    total = reduced[:, pl.ds(trc * share, share)]
+    for copy in sum_copies:
+        copy.wait_recv()
     for step in range(1, groups_trc):
-        target = lax.rem(trc + step, groups_trc)
-        copy = pltpu.make_async_remote_copy(
-            src_ref=reduced.at[:, pl.ds(target * share, share)],
-            dst_ref=arrived.at[step - 1],
-            send_sem=sum_send.at[step - 1],
-            recv_sem=sum_recv.at[step - 1],
-            device_id={"trc": target},
-            device_id_type=MESH,
-        )
-        copy.start()
-        sum_copies.append(copy)
-    total = reduced[:, pl.ds(trc * share, share)]
-    for step, copy in enumerate(sum_copies):
-        copy.wait_recv()
-        total = total + arrived[step]
+        total = total + arrived[step - 1]
     speed_ref[...] = total
 
     for copies in [field_copies] + first_copies + cot_copies + middle_copies + back_copies:
@@ -569,7 +625,7 @@
             jax.ShapeDtypeStruct(flat, jnp.float32),
             jax.ShapeDtypeStruct((3, share, columns, lanes), jnp.float32),
         ),
-        in_specs=[pl.BlockSpec(memory_space=pltpu.VMEM)] * 8,
+        in_specs=[pl.BlockSpec(memory_space=pltpu.HBM)] * 8,
         out_specs=(pl.BlockSpec(memory_space=pltpu.VMEM),) * 2,
         scratch_shapes=[
             extended,
@@ -591,8 +647,13 @@
             pltpu.SemaphoreType.DMA((4, groups, 4)),
             pltpu.SemaphoreType.DMA((2, 4)),
             pltpu.SemaphoreType.DMA((2, 4)),
-            pltpu.SemaphoreType.DMA((max(sizes[2] - 1, 1),)),
-            pltpu.SemaphoreType.DMA((max(sizes[2] - 1, 1),)),
+            pltpu.SemaphoreType.DMA((2, max(sizes[2] - 1, 1))),
+            pltpu.SemaphoreType.DMA((2, max(sizes[2] - 1, 1))),
+            pltpu.VMEM((groups, levels, columns, ROWS, lanes), jnp.float32),
+            pltpu.SemaphoreType.DMA((8,)),
+            pltpu.VMEM(flat, jnp.float32),
+            pltpu.VMEM(flat, jnp.float32),
+            *[pltpu.VMEM(values.shape, values.dtype) for values in fields],
         ],
         compiler_params=pltpu.CompilerParams(
             collective_id=0, has_side_effects=True, vmem_limit_bytes=48 * 1024 * 1024

time: 36.6 us -> 35.5 us (0.970)
  Pallas kernels: 27.4 us -> 26.3 us
    pallas_call x1, Pallas kernels: 27.4 us -> 26.3 us  [body(): pl.pallas_call(functools.partial(kernel, sizes, tracers.shape), out_shape...]
where the time goes in v2:
time: 35.5 us; the launch traced here: 34.9 us
  Pallas kernels  26.3 us (74%)
  local copies, waits for them, and re-layouts  7.96 us (22%)
  between operations  0.66 us (2%)
    pallas_call x1, Pallas kernels, body(): pl.pallas_call(functools.partial(kernel, sizes, tracers.shape), out_shape...  26.3 us
    unnamed x18, local copies, waits for them, and re-layouts  7.96 us

profile of v2, /device:TPU:0, one launch (start us, length us, event | category | flops | bytes accessed | tf_op | source)
XLA Modules:
  0.0 34.9 jit_solution(9625690947433882717)
XLA Ops:
  0.6 0.0 copy-start
  0.6 1.0 %copy-done = f32[16,8,8,128]{3,2,1,0:T(8,128)S(1)} copy-done((f32[16,8,8,128]{3,2,1,0:T(8,128)S(1)}, f32[16,8,8,128]{3,2,1,0:T(8,128)}, u32[]{:S(2)}) %copy-start) | copy-done | bytes 524312
  1.7 0.0 copy-start.1
  1.7 1.0 %copy-done.1 = f32[16,8,8,128]{3,2,1,0:T(8,128)S(1)} copy-done((f32[16,8,8,128]{3,2,1,0:T(8,128)S(1)}, f32[16,8,8,128]{3,2,1,0:T(8,128)}, u32[]{:S(2)}) %copy-start.1) | copy-done | bytes 524312
  2.7 0.0 copy-start.2
  2.7 0.8 %copy-done.2 = f32[8,8,128]{2,1,0:T(8,128)S(1)} copy-done((f32[8,8,128]{2,1,0:T(8,128)S(1)}, f32[8,8,128]{2,1,0:T(8,128)}, u32[]{:S(2)}) %copy-start.2) | copy-done | bytes 32792
  3.5 0.0 copy-start.3
  3.5 0.8 %copy-done.3 = f32[8,8,128]{2,1,0:T(8,128)S(1)} copy-done((f32[8,8,128]{2,1,0:T(8,128)S(1)}, f32[8,8,128]{2,1,0:T(8,128)}, u32[]{:S(2)}) %copy-start.3) | copy-done | bytes 32792
  4.2 0.0 copy-start.4
  4.2 0.8 %copy-done.4 = f32[8,8,128]{2,1,0:T(8,128)S(1)} copy-done((f32[8,8,128]{2,1,0:T(8,128)S(1)}, f32[8,8,128]{2,1,0:T(8,128)}, u32[]{:S(2)}) %copy-start.4) | copy-done | bytes 32792
  5.0 0.0 copy-start.5
  5.0 0.8 %copy-done.5 = f32[8,8,128]{2,1,0:T(8,128)S(1)} copy-done((f32[8,8,128]{2,1,0:T(8,128)S(1)}, f32[8,8,128]{2,1,0:T(8,128)}, u32[]{:S(2)}) %copy-start.5) | copy-done | bytes 32792
  5.8 0.0 copy-start.6
  5.8 0.8 %copy-done.6 = f32[8,8,128]{2,1,0:T(8,128)S(1)} copy-done((f32[8,8,128]{2,1,0:T(8,128)S(1)}, f32[8,8,128]{2,1,0:T(8,128)}, u32[]{:S(2)}) %copy-start.6) | copy-done | bytes 32792
  6.5 0.0 copy-start.7
  6.5 0.7 %copy-done.7 = s32[8,128]{1,0:T(8,128)S(1)} copy-done((s32[8,128]{1,0:T(8,128)S(1)}, s32[8,128]{1,0:T(8,128)}, u32[]{:S(2)}) %copy-start.7) | copy-done | bytes 4120
  7.2 26.3 %shard_map.95 = (f32[1024,128]{1,0:T(8,128)S(1)}, f32[3,4,8,128]{3,2,1,0:T(8,128)S(1)}) custom-call(f32[1024,128]{1,0:T(8,128)S(1)} %bitcast.3, f32[1024,128]{1,0:T(8,128)S(1)} %bitcast.4, f32[8,8,128]{2,1,0:T(8,128)S(1)} %copy-done.2, f32[8,8,128]{2,1,0:T(8,128)S(1)} %copy-done.3, f32[8,8,128]{2,1,0:T(8,128)S(1)} %copy-done.4, f32[8,8,128]{2,1,0:T(8,128)S(1)} %copy-done.5, ...), custom_call_target="tpu_custom_call" | custom-call | tf_op jit(solution)/shard_map/pallas_call | solution.py:622
  33.5 0.8 %copy.12 = f32[16,8,8,128]{3,2,1,0:T(8,128)} copy(f32[16,8,8,128]{3,2,1,0:T(8,128)S(1)} %bitcast.5) | data formatting | bytes 1048576
  34.3 0.6 %copy.13 = f32[3,4,8,128]{3,2,1,0:T(8,128)} copy(f32[3,4,8,128]{3,2,1,0:T(8,128)S(1)} %get-tuple-element.9) | data formatting | bytes 98304
Async XLA Ops:
  0.6 1.0 %copy-start = (f32[16,8,8,128]{3,2,1,0:T(8,128)S(1)}, f32[16,8,8,128]{3,2,1,0:T(8,128)}, u32[]{:S(2)}) copy-start(f32[16,8,8,128]{3,2,1,0:T(8,128)} %param.8) | copy-start | bytes 1572868
  1.7 1.0 %copy-start.1 = (f32[16,8,8,128]{3,2,1,0:T(8,128)S(1)}, f32[16,8,8,128]{3,2,1,0:T(8,128)}, u32[]{:S(2)}) copy-start(f32[16,8,8,128]{3,2,1,0:T(8,128)} %param.9) | copy-start | bytes 1572868
  2.7 0.8 %copy-start.2 = (f32[8,8,128]{2,1,0:T(8,128)S(1)}, f32[8,8,128]{2,1,0:T(8,128)}, u32[]{:S(2)}) copy-start(f32[8,8,128]{2,1,0:T(8,128)} %zonal_hbm.1) | copy-start | bytes 98308
  3.5 0.8 %copy-start.3 = (f32[8,8,128]{2,1,0:T(8,128)S(1)}, f32[8,8,128]{2,1,0:T(8,128)}, u32[]{:S(2)}) copy-start(f32[8,8,128]{2,1,0:T(8,128)} %merid_hbm.1) | copy-start | bytes 98308
  4.2 0.8 %copy-start.4 = (f32[8,8,128]{2,1,0:T(8,128)S(1)}, f32[8,8,128]{2,1,0:T(8,128)}, u32[]{:S(2)}) copy-start(f32[8,8,128]{2,1,0:T(8,128)} %vert_hbm.1) | copy-start | bytes 98308
  5.0 0.8 %copy-start.5 = (f32[8,8,128]{2,1,0:T(8,128)S(1)}, f32[8,8,128]{2,1,0:T(8,128)}, u32[]{:S(2)}) copy-start(f32[8,8,128]{2,1,0:T(8,128)} %lateral_hbm.1) | copy-start | bytes 98308
  5.8 0.8 %copy-start.6 = (f32[8,8,128]{2,1,0:T(8,128)S(1)}, f32[8,8,128]{2,1,0:T(8,128)}, u32[]{:S(2)}) copy-start(f32[8,8,128]{2,1,0:T(8,128)} %vmix_hbm.1) | copy-start | bytes 98308
  6.5 0.7 %copy-start.7 = (s32[8,128]{1,0:T(8,128)S(1)}, s32[8,128]{1,0:T(8,128)}, u32[]{:S(2)}) copy-start(s32[8,128]{1,0:T(8,128)} %depth_hbm.1) | copy-start | bytes 12292

commit v3 on v2

--- a/solution.py
+++ b/solution.py
@@ -27,18 +27,29 @@
     return step * (step + step) + ALBADA_FLOOR
 
 
-def forward_line(count, q, rise, fall, spread, emit):
+def slopes(lower, upper, slope, half_inverse, total):
+    fourfold = 4.0 * slope
+    by_lower = (upper * (lower + total) - lower * fourfold) * half_inverse
+    by_upper = (lower * (upper + total) - upper * fourfold) * half_inverse
+    return by_lower, by_upper
+
+
+def forward_line(count, q, rise, fall, spread, emit, keep, keep_face):
     values = {x: q(x) for x in range(-2, count + 2)}
     steps = {c: values[c] - values[c - 1] for c in range(-1, count + 2)}
     squares = {c: doubled_square(steps[c]) for c in steps}
     through = {}
     above = None
     for x in range(-1, count + 1):
-        slope, _, _ = limiter(steps[x], steps[x + 1], squares[x], squares[x + 1])
+        parts = limiter(steps[x], steps[x + 1], squares[x], squares[x + 1])
+        slope = parts[0]
+        keep(x, *slopes(steps[x], steps[x + 1], *parts))
         if x >= 0:
-            through[x] = (
-                rise(x) * above + fall(x) * (values[x] - slope) - spread(x) * steps[x]
-            )
+            falls = fall(x)
+            carried = jnp.where(falls < 0.0, values[x] - slope, above)
+            through[x] = (rise(x) + falls) * carried - spread(x) * steps[x]
+            if x < count:
+                keep_face(x, carried)
         above = values[x] + slope
         if x >= 1:
             emit(x - 1, through[x - 1] - through[x])
@@ -75,6 +86,24 @@
             emit(x - 1, (jump[x - 1] - jump[x]) + (up[x] + down[x - 1]))
 
 
+def early_line(count, g, kept, carried, rise, fall, spread, emit, speed):
+    cots = {x: g(x) for x in range(-2, count + 2)}
+    faces = {c: cots[c] - cots[c - 1] for c in range(-1, count + 2)}
+    up = {c: faces[c] * rise(c) for c in range(0, count + 2)}
+    down = {c: faces[c] * fall(c) for c in range(-1, count + 1)}
+    jump, later = {}, None
+    for x in range(-1, count + 1):
+        weight = up[x + 1] - down[x]
+        if x >= 0:
+            jump[x] = kept(0, x) * weight + later - spread(x) * faces[x]
+        if x < count:
+            later = kept(1, x) * weight
+        if 0 <= x < count:
+            speed(x, faces[x] * carried(x))
+        if x >= 1:
+            emit(x - 1, (jump[x - 1] - jump[x]) + (up[x] + down[x - 1]))
+
+
 def across(values, lane, last):
     before = jnp.where(lane == 0, 0.0, pltpu.roll(values, 1, 1))
     lower = values - before
@@ -84,10 +113,13 @@
 
 def forward_cell(values, rise, fall, spread, lane, last):
     lower, upper = across(values, lane, last)
-    slope, _, _ = limiter(lower, upper, doubled_square(lower), doubled_square(upper))
+    parts = limiter(lower, upper, doubled_square(lower), doubled_square(upper))
+    slope = parts[0]
     above = pltpu.roll(values + slope, 1, 1)
-    through = rise * above + fall * (values - slope) - spread * lower
-    return through - pltpu.roll(through, last, 1)
+    carried = jnp.where(fall < 0.0, values - slope, above)
+    through = (rise + fall) * carried - spread * lower
+    kept = slopes(lower, upper, *parts)
+    return through - pltpu.roll(through, last, 1), kept, carried
 
 
 def backward_cell(values, cot, rise, fall, spread, lane, last):
@@ -112,6 +144,24 @@
         - jnp.where(lane == last, 0.0, pltpu.roll(near, last, 1))
     )
     carried = jnp.where(fall < 0.0, values - slope, pltpu.roll(values + slope, 1, 1))
+    return result, face * carried
+
+
+def early_cell(cot, by_lower, by_upper, carried, rise, fall, spread, lane, last):
+    face = cot - pltpu.roll(cot, 1, 1)
+    up = pltpu.roll(face * rise, last, 1)
+    down = face * fall
+    weight = up - down
+    later = by_upper * weight
+    near = by_lower * weight - spread * face
+    result = (
+        near
+        - later
+        + up
+        + down
+        + jnp.where(lane == 0, 0.0, pltpu.roll(later, 1, 1))
+        - jnp.where(lane == last, 0.0, pltpu.roll(near, last, 1))
+    )
     return result, face * carried
 
 
@@ -150,6 +200,10 @@
     sum_send,
     sum_recv,
     start_sum,
+    kept_zonal,
+    kept_vert,
+    kept_merid,
+    carried_all,
     load_sem,
     *loaded,
 ):
@@ -387,7 +441,7 @@
         def step(l, carry):
             for i in range(columns):
                 values = first[g, l + 2, i + 2]
-                middle[g, l + 2, i + 2] = values + forward_cell(
+                gain, kept, carried = forward_cell(
                     values,
                     merid_fields[0, l, i],
                     merid_fields[1, l, i],
@@ -395,6 +449,10 @@
                     lane,
                     end,
                 )
+                middle[g, l + 2, i + 2] = values + gain
+                kept_merid[0, g, l, i] = kept[0]
+                kept_merid[1, g, l, i] = kept[1]
+                carried_all[1, g, l, i] = carried
             return carry
 
         lax.fori_loop(0, levels, step, 0)
@@ -431,6 +489,13 @@
             def emit(x, value):
                 middle[g, l + 2, x + 2] += value
 
+            def keep(x, by_lower, by_upper):
+                kept_zonal[0, g, l, x + 1] = by_lower
+                kept_zonal[1, g, l, x + 1] = by_upper
+
+            def keep_face(c, value):
+                carried_all[0, g, l, c] = value
+
             forward_line(
                 columns,
                 lambda x: first[g, l + 2, x + 2],
@@ -438,6 +503,8 @@
                 lambda c: zonal_fields[1, l, c + 1],
                 lambda c: zonal_fields[2, l, c + 1],
                 emit,
+                keep,
+                keep_face,
             )
             return carry
 
@@ -447,6 +514,13 @@
         def step(i, carry):
             def emit(x, value):
                 middle[g, x + 2, i + 2] += value
+
+            def keep(x, by_lower, by_upper):
+                kept_vert[0, g, x + 1, i] = by_lower
+                kept_vert[1, g, x + 1, i] = by_upper
+
+            def keep_face(c, value):
+                carried_all[2, g, c, i] = value
 
             forward_line(
                 levels,
@@ -455,6 +529,8 @@
                 lambda c: vert_fields[1, c + 1, i],
                 lambda c: vert_fields[2, c + 1, i],
                 emit,
+                keep,
+                keep_face,
             )
             return carry
 
@@ -479,10 +555,8 @@
 
         lax.fori_loop(0, levels, step, 0)
 
-    def pull_zonal(state, cot, store, g, fresh, begin=0, count=levels):
-        def step(index, carry):
-            l = lax.rem(begin + index, levels)
-
+    def pull_zonal(state, cot, store, g, fresh):
+        def step(l, carry):
             def speed(c, value):
                 sums[0, l, c] = value if fresh else sums[0, l, c] + value
 
@@ -498,7 +572,7 @@
             )
             return carry
 
-        lax.fori_loop(0, count, step, 0)
+        lax.fori_loop(0, levels, step, 0)
 
     def pull_vert(state, cot, store, g, fresh):
         def step(i, carry):
@@ -519,21 +593,81 @@
 
         lax.fori_loop(0, columns, step, 0)
 
+    def early_merid(g):
+        def step(l, carry):
+            for i in range(columns):
+                own_cot = middle_cot[g, l + 2, i + 2]
+                pulled, share = early_cell(
+                    own_cot,
+                    kept_merid[0, g, l, i],
+                    kept_merid[1, g, l, i],
+                    carried_all[1, g, l, i],
+                    merid_fields[0, l, i],
+                    merid_fields[1, l, i],
+                    merid_fields[2, l, i],
+                    lane,
+                    end,
+                )
+                start_sum[g, l, i] = own_cot + pulled
+                sums[1, l, i] += share
+            return carry
+
+        lax.fori_loop(0, levels, step, 0)
+
+    def early_zonal(g, begin, count):
+        def step(index, carry):
+            l = lax.rem(begin + index, levels)
+
+            def speed(c, value):
+                sums[0, l, c] += value
+
+            def emit(i, value):
+                rows = pl.ds(g * ROWS * cells + l * columns + i, ROWS, stride=cells)
+                start_ref[rows, :] = start_sum[g, l, i] + value
+
+            early_line(
+                columns,
+                lambda x: middle_cot[g, l + 2, x + 2],
+                lambda kind, x: kept_zonal[kind, g, l, x + 1],
+                lambda c: carried_all[0, g, l, c],
+                lambda c: zonal_fields[0, l, c + 1],
+                lambda c: zonal_fields[1, l, c + 1],
+                lambda c: zonal_fields[2, l, c + 1],
+                emit,
+                speed,
+            )
+            return carry
+
+        lax.fori_loop(0, count, step, 0)
+
+    def early_vert(g):
+        def step(i, carry):
+            def speed(c, value):
+                sums[2, c, i] += value
+
+            def emit(l, value):
+                start_sum[g, l, i] += value
+
+            early_line(
+                levels,
+                lambda x: middle_cot[g, x + 2, i + 2],
+                lambda kind, x: kept_vert[kind, g, x + 1, i],
+                lambda c: carried_all[2, g, c, i],
+                lambda c: vert_fields[0, c + 1, i],
+                lambda c: vert_fields[1, c + 1, i],
+                lambda c: vert_fields[2, c + 1, i],
+                emit,
+                speed,
+            )
+            return carry
+
+        lax.fori_loop(0, columns, step, 0)
+
     def store_middle(g, l, i, value, fresh):
         if fresh:
             middle_cot[g, l + 2, i + 2] = value
         else:
             middle_cot[g, l + 2, i + 2] += value
-
-    def store_start(g, l, i, value, fresh):
-        if fresh:
-            start_sum[g, l, i] = value
-        else:
-            start_sum[g, l, i] += value
-
-    def store_last(g, l, i, value, fresh):
-        rows = pl.ds(g * ROWS * cells + l * columns + i, ROWS, stride=cells)
-        start_ref[rows, :] = start_sum[g, l, i] + value
 
     for g in range(groups):
         arrive(first_copies[g], ("lev",))
@@ -556,10 +690,10 @@
         pull_zonal(middle, last_cot, store_middle, g, g == 0)
         start(back_copies[g])
     for g in range(groups):
-        pull_merid(first, middle_cot, store_start, g, False)
+        early_merid(g)
     for g in range(groups):
         arrive(back_copies[g], ("lev",))
-        pull_vert(first, middle_cot, store_start, g, False)
+        early_vert(g)
 
     share = levels // groups_trc
     sum_copies = []
@@ -594,11 +728,11 @@
     after = (trc + 1) * share
     if groups_trc > 1:
         for g in range(groups):
-            pull_zonal(first, middle_cot, store_last, g, False, after, levels - share)
+            early_zonal(g, after, levels - share)
         reduce_rows((0,), after, levels - share)
         send_rows(1, pl.ds(0, 1))
     for g in range(groups):
-        pull_zonal(first, middle_cot, store_last, g, False, trc * share, share)
+        early_zonal(g, trc * share, share)
     reduce_rows((0,), trc * share, share)
     total = reduced[:, pl.ds(trc * share, share)]
     for copy in sum_copies:
@@ -650,13 +784,17 @@
             pltpu.SemaphoreType.DMA((2, max(sizes[2] - 1, 1))),
             pltpu.SemaphoreType.DMA((2, max(sizes[2] - 1, 1))),
             pltpu.VMEM((groups, levels, columns, ROWS, lanes), jnp.float32),
+            pltpu.VMEM((2, groups, levels, columns + 2, ROWS, lanes), jnp.float32),
+            pltpu.VMEM((2, groups, levels + 2, columns, ROWS, lanes), jnp.float32),
+            pltpu.VMEM((2, groups, levels, columns, ROWS, lanes), jnp.float32),
+            pltpu.VMEM((3, groups, levels, columns, ROWS, lanes), jnp.float32),
             pltpu.SemaphoreType.DMA((8,)),
             pltpu.VMEM(flat, jnp.float32),
             pltpu.VMEM(flat, jnp.float32),
             *[pltpu.VMEM(values.shape, values.dtype) for values in fields],
         ],
         compiler_params=pltpu.CompilerParams(
-            collective_id=0, has_side_effects=True, vmem_limit_bytes=48 * 1024 * 1024
+            collective_id=0, has_side_effects=True, vmem_limit_bytes=60 * 1024 * 1024
         ),
     )(tracers.reshape(flat), cotangent.reshape(flat), *fields)
     return start_cot.reshape(tracers.shape), speed_cot

time: 35.5 us -> 30.2 us (0.85); the launches traced: 34.9 us -> 30 us
  local copies, waits for them, and re-layouts: 7.96 us -> 2.52 us
  Pallas kernels: 26.3 us -> 26.8 us
    unnamed x18 -> x4, local copies, waits for them, and re-layouts: 7.96 us -> 2.52 us
    pallas_call x1, Pallas kernels: 26.3 us -> 26.8 us  [body(): pl.pallas_call(functools.partial(kernel, sizes, tracers.shape), out_shape...]
where the time goes in v3:
time: 30.2 us; the launch traced here: 30 us
  Pallas kernels  26.8 us (89%)
  local copies, waits for them, and re-layouts  2.52 us (8%)
  between operations  0.65 us (2%)
    pallas_call x1, Pallas kernels, body(): pl.pallas_call(functools.partial(kernel, sizes, tracers.shape), out_shape...  26.8 us
    unnamed x4, local copies, waits for them, and re-layouts  2.52 us

profile of v3, /device:TPU:0, one launch (start us, length us, event | category | flops | bytes accessed | tf_op | source)
XLA Modules:
  0.0 30.0 jit_solution(14119807643188013748)
XLA Ops:
  0.6 26.8 %shard_map.95 = (f32[1024,128]{1,0:T(8,128)}, f32[3,4,8,128]{3,2,1,0:T(8,128)}) custom-call(f32[1024,128]{1,0:T(8,128)} %bitcast.3, f32[1024,128]{1,0:T(8,128)} %bitcast.4, f32[8,8,128]{2,1,0:T(8,128)} %zonal_hbm.1, f32[8,8,128]{2,1,0:T(8,128)} %merid_hbm.1, f32[8,8,128]{2,1,0:T(8,128)} %vert_hbm.1, f32[8,8,128]{2,1,0:T(8,128)} %lateral_hbm.1, ...), custom_call_target="tpu_custom_call" | custom-call | tf_op jit(solution)/shard_map/pallas_call | solution.py:756
  27.5 0.0 copy-start
  27.5 1.9 %copy.12 = f32[16,8,8,128]{3,2,1,0:T(8,128)} copy(f32[16,8,8,128]{3,2,1,0:T(8,128)} %bitcast.5) | data formatting | bytes 1048576
  29.4 0.0 copy-done
  29.4 0.6 %copy.13 = f32[3,4,8,128]{3,2,1,0:T(8,128)} copy(f32[3,4,8,128]{3,2,1,0:T(8,128)S(1)} %copy-done) | data formatting | bytes 98304
Async XLA Ops:
  27.5 1.9 %copy-start = (f32[3,4,8,128]{3,2,1,0:T(8,128)S(1)}, f32[3,4,8,128]{3,2,1,0:T(8,128)}, u32[]{:S(2)}) copy-start(f32[3,4,8,128]{3,2,1,0:T(8,128)} %get-tuple-element.9) | copy-start | bytes 147460

commit v4 on v3

--- a/solution.py
+++ b/solution.py
@@ -455,7 +455,7 @@
                 carried_all[1, g, l, i] = carried
             return carry
 
-        lax.fori_loop(0, levels, step, 0)
+        lax.fori_loop(0, levels, step, 0, unroll=2)
 
     for g in range(groups):
         forward_merid(g)
@@ -508,7 +508,7 @@
             )
             return carry
 
-        lax.fori_loop(0, levels, step, 0)
+        lax.fori_loop(0, levels, step, 0, unroll=2)
 
     def forward_vert(g):
         def step(i, carry):
@@ -534,7 +534,7 @@
             )
             return carry
 
-        lax.fori_loop(0, columns, step, 0)
+        lax.fori_loop(0, columns, step, 0, unroll=2)
 
     def pull_merid(state, cot, store, g, fresh):
         def step(l, carry):
@@ -553,7 +553,7 @@
                 sums[1, l, i] = share if fresh else sums[1, l, i] + share
             return carry
 
-        lax.fori_loop(0, levels, step, 0)
+        lax.fori_loop(0, levels, step, 0, unroll=2)
 
     def pull_zonal(state, cot, store, g, fresh):
         def step(l, carry):
@@ -572,7 +572,7 @@
             )
             return carry
 
-        lax.fori_loop(0, levels, step, 0)
+        lax.fori_loop(0, levels, step, 0, unroll=2)
 
     def pull_vert(state, cot, store, g, fresh):
         def step(i, carry):
@@ -591,7 +591,7 @@
             )
             return carry
 
-        lax.fori_loop(0, columns, step, 0)
+        lax.fori_loop(0, columns, step, 0, unroll=2)
 
     def early_merid(g):
         def step(l, carry):
@@ -612,7 +612,7 @@
                 sums[1, l, i] += share
             return carry
 
-        lax.fori_loop(0, levels, step, 0)
+        lax.fori_loop(0, levels, step, 0, unroll=2)
 
     def early_zonal(g, begin, count):
         def step(index, carry):
@@ -638,7 +638,7 @@
             )
             return carry
 
-        lax.fori_loop(0, count, step, 0)
+        lax.fori_loop(0, count, step, 0, unroll=2)
 
     def early_vert(g):
         def step(i, carry):
@@ -661,7 +661,7 @@
             )
             return carry
 
-        lax.fori_loop(0, columns, step, 0)
+        lax.fori_loop(0, columns, step, 0, unroll=2)
 
     def store_middle(g, l, i, value, fresh):
         if fresh:
@@ -705,7 +705,7 @@
                 reduced[row, l] = opened_all[row, l] * jnp.sum(sums[row, l], axis=1)
             return carry
 
-        lax.fori_loop(0, count, step, 0)
+        lax.fori_loop(0, count, step, 0, unroll=2)
 
     def send_rows(part, rows):
         for step in range(1, groups_trc):

time: 30.2 us -> 27.7 us (0.917)
  Pallas kernels: 26.8 us -> 24.4 us
    pallas_call x1, Pallas kernels: 26.8 us -> 24.4 us  [body(): pl.pallas_call(functools.partial(kernel, sizes, tracers.shape), out_shape...]
where the time goes in v4:
time: 27.7 us; the launch traced here: 27.6 us
  Pallas kernels  24.4 us (88%)
  local copies, waits for them, and re-layouts  2.52 us (9%)
  between operations  0.65 us (2%)
    pallas_call x1, Pallas kernels, body(): pl.pallas_call(functools.partial(kernel, sizes, tracers.shape), out_shape...  24.4 us
    unnamed x4, local copies, waits for them, and re-layouts  2.52 us

profile of v4, /device:TPU:0, one launch (start us, length us, event | category | flops | bytes accessed | tf_op | source)
XLA Modules:
  0.0 27.6 jit_solution(13842295847825993930)
XLA Ops:
  0.6 24.4 %shard_map.95 = (f32[1024,128]{1,0:T(8,128)}, f32[3,4,8,128]{3,2,1,0:T(8,128)}) custom-call(f32[1024,128]{1,0:T(8,128)} %bitcast.3, f32[1024,128]{1,0:T(8,128)} %bitcast.4, f32[8,8,128]{2,1,0:T(8,128)} %zonal_hbm.1, f32[8,8,128]{2,1,0:T(8,128)} %merid_hbm.1, f32[8,8,128]{2,1,0:T(8,128)} %vert_hbm.1, f32[8,8,128]{2,1,0:T(8,128)} %lateral_hbm.1, ...), custom_call_target="tpu_custom_call" | custom-call | tf_op jit(solution)/shard_map/pallas_call | solution.py:756
  25.0 0.0 copy-start
  25.1 1.9 %copy.12 = f32[16,8,8,128]{3,2,1,0:T(8,128)} copy(f32[16,8,8,128]{3,2,1,0:T(8,128)} %bitcast.5) | data formatting | bytes 1048576
  26.9 0.0 copy-done
  27.0 0.6 %copy.13 = f32[3,4,8,128]{3,2,1,0:T(8,128)} copy(f32[3,4,8,128]{3,2,1,0:T(8,128)S(1)} %copy-done) | data formatting | bytes 98304
Async XLA Ops:
  25.0 1.9 %copy-start = (f32[3,4,8,128]{3,2,1,0:T(8,128)S(1)}, f32[3,4,8,128]{3,2,1,0:T(8,128)}, u32[]{:S(2)}) copy-start(f32[3,4,8,128]{3,2,1,0:T(8,128)} %get-tuple-element.9) | copy-start | bytes 147460
